TPU v7x, 32 devices: a whole 2x2x4 slice. The times are simulated.
32 devices in a mesh: row: 16 (over z, x, core), col: 2 (over y).
Axes of the slice: x: 2, y: 2, z: 4, core: 2. Of those that a mesh axis runs over, the one named last changes fastest.
Arguments:
- vectors: bfloat16 [8, 32768], P(None, ('row', 'col')), may hold values from -6 to 6
- energies: float32 [32768], P(('row', 'col')), may hold values from 0.5 to 6
- tiles: bfloat16 [32768, 4096], P(('row', 'col')), may hold values from -0.25 to 0.25
- tile_rows: int32 [32768], P(('row', 'col')), may hold values from 0 to 31, as said below
- tile_cols: int32 [32768], P(('row', 'col')), may hold values from 0 to 255
- tile_count: int32 [32], P(('row', 'col')), may hold values from 128 to 1024, as said below
Outputs:
- product: bfloat16 [8, 32768], P(None, ('row', 'col'))
- residual: float32 [8, 32768], P(None, ('row', 'col'))
Inputs may be any that keep to these rules, and one draw needn't show every extreme that they name: `tile_count`: every count is at least 128, and some device uses all 1024 slots in every draw; a few devices are full while most use far fewer. `tile_rows`: slots may name the same row and column block more than once; such tiles add.
All inputs are finite; a program needn't handle non-finite values.
Results may differ from a plain program's by a relative error of at most 0.008.
Values may be sent and summed in bfloat16 or wider, within the bound.
No kernel may reach another device: no remote copies, remote signals or barrier semaphores. Data moves between devices by JAX's collectives and lax.ppermute only.
A program may use at most 64 MiB of HBM per device.

v0:
```python
import functools
import math

import jax
import jax.numpy as jnp
from jax import lax
from jax.experimental import pallas as pl
from jax.experimental.pallas import tpu as pltpu
from jax.sharding import Mesh, PartitionSpec as P

LANES = 128
SUB = 8
CHUNK = 128

NT = (((1,), (1,)), ((), ()))


def tile_kernel(
    n_core, n_col, side, count_s, rows_h, cols_h, ener_h, tiles, *refs,
):
    gath, refs = refs[:n_core], refs[n_core:]
    (own_ref, send_ref, rest_ref, rows_s, cols_s, ener,
     buf, table, picked, select, part, sems, small, *acc) = refs
    n_far, kvec, own = gath[0].shape
    slots = tiles.shape[0]
    blk_own = own // side
    per = LANES // side
    n_chunk = tiles.shape[1] // LANES
    my_far, my_core, my_col = (lax.axis_index(name) for name in ("far", "core", "col"))

    copies = [
        pltpu.make_async_copy(src, dst, small.at[i])
        for i, (src, dst) in enumerate(
            ((cols_h, cols_s), (rows_h, rows_s), (ener_h, ener))
        )
    ]
    for copy in copies:
        copy.start()

    def tile_copy(ch):
        span = pl.ds(pl.multiple_of(ch * CHUNK, CHUNK), CHUNK)
        return pltpu.make_async_copy(tiles.at[span], buf.at[span], sems.at[ch])

    count = count_s[0]
    used = (count + CHUNK - 1) // CHUNK

    def start(ch, carry):
        tile_copy(ch).start()
        return carry

    lax.fori_loop(0, used, start, 0)

    lane = lax.broadcasted_iota(jnp.int32, (kvec, LANES), 1)
    low = lane < side
    zero = jnp.zeros((kvec, LANES), jnp.float32)

    for s in range(n_core):
        core = lax.rem(my_core + (n_core - s), n_core)
        for f in range(n_far):
            for p in range(own // LANES):
                x = gath[s][f, :, p * LANES:(p + 1) * LANES].astype(jnp.float32)
                y = pltpu.roll(x, side, 1)
                at = (f * n_core + core) * blk_own + p * per
                even = jnp.concatenate([jnp.where(low, x, zero), jnp.where(low, zero, y)], axis=0)
                odd = jnp.concatenate([jnp.where(low, y, zero), jnp.where(low, zero, x)], axis=0)
                table[at] = even
                table[at + 1] = odd
    n_blocks = n_far * n_core * blk_own
    table[n_blocks] = jnp.zeros((per * kvec, LANES), jnp.float32)

    for copy in copies:
        copy.wait()
    n_seg = acc[0].shape[0]
    width = n_chunk * SUB

    def clear(r, carry):
        for a in acc:
            a[r] = jnp.zeros(a.shape[1:], jnp.float32)
        return carry

    lax.fori_loop(0, n_seg, clear, 0)

    k_id = lax.broadcasted_iota(jnp.int32, (width, LANES), 0)
    n_id = lax.broadcasted_iota(jnp.int32, (width, LANES), 1)
    base_id = n_id - per * (k_id // SUB)
    for par in range(per):
        for jp in range(per):
            at = (par * per + jp) * width
            hit = (base_id == side * par + jp).astype(jnp.float32)
            select[at:at + width, :] = hit.astype(jnp.bfloat16)

    rows_of = per * kvec

    def product(base, half, x, check):
        xh = x[half * SUB:(half + 1) * SUB]
        w = jnp.concatenate(
            [xh[:, c * LANES:(c + 1) * LANES] for c in range(n_chunk)], axis=0
        ).astype(jnp.bfloat16)
        entries = []
        for t in range(SUB):
            slot = base + half * SUB + t
            at = cols_s[slot]
            entries.append(table[jnp.where(slot < count, at, n_blocks) if check else at])
        left = jnp.concatenate(entries, axis=0).astype(jnp.bfloat16)
        return lax.dot_general(left, w, NT, preferred_element_type=jnp.float32)

    def accumulate(at, out):
        for t in range(SUB):
            r = rows_s[at + t]
            acc[t][r] += out[t * rows_of:(t + 1) * rows_of]

    def one_chunk(ch, check):
        tile_copy(ch).wait()
        waiting = None
        for q in range(CHUNK // (2 * SUB)):
            base = pl.multiple_of(ch * CHUNK + q * 2 * SUB, 2 * SUB)
            x = buf[pl.ds(base, 2 * SUB), :].astype(jnp.float32)
            for half in range(2):
                out = product(base, half, x, check)
                if waiting is not None:
                    accumulate(*waiting)
                waiting = (base + half * SUB, out)
        accumulate(*waiting)

    def full_chunk(ch, carry):
        one_chunk(ch, False)
        return carry

    lax.fori_loop(0, count // CHUNK, full_chunk, 0)

    @pl.when(used > count // CHUNK)
    def _():
        one_chunk(used - 1, True)

    lane_w = lax.broadcasted_iota(jnp.int32, (rows_of, width), 1) % SUB
    pairs = n_seg // per

    def pick(m, carry):
        pieces = []
        for par in range(per):
            total = jnp.zeros((rows_of, width), jnp.float32)
            for t in range(SUB):
                total = jnp.where(lane_w == t, acc[t][m * per + par], total)
            for jp in range(per):
                pieces.append(total[jp * kvec:(jp + 1) * kvec])
        a = jnp.concatenate(pieces, axis=1)
        hi = a.astype(jnp.bfloat16).astype(jnp.float32)
        both = jnp.concatenate([hi, a - hi], axis=0).astype(jnp.bfloat16)
        picked[pl.ds(pl.multiple_of(m * 2 * kvec, 2 * kvec), 2 * kvec), :] = both
        return carry

    lax.fori_loop(0, pairs, pick, 0)

    spread = jnp.dot(picked[...], select[...], preferred_element_type=jnp.float32)
    for m in range(pairs):
        at = m * 2 * kvec
        row = spread[at:at + kvec] + spread[at + kvec:at + 2 * kvec]
        c, lane0 = divmod(m * LANES, own)
        part[c, :, lane0:lane0 + LANES] = row

    own_ref[...] = part[my_col] + ener[...] * gath[0][my_far].astype(jnp.float32)
    for s in range(1, n_col):
        share = part[lax.rem(my_col + s, n_col)]
        send_ref[s - 1] = share.astype(jnp.bfloat16)
        rest_ref[s - 1] = share


def tile_work(rows, cols, count, gath, n_col, ener, tiles):
    n_core = len(gath)
    n_far, kvec, own = gath[0].shape
    slots, area = tiles.shape
    side = math.isqrt(area)
    per = LANES // side
    blk_own = own // side
    n_seg = n_col * blk_own
    width = area // LANES * SUB
    vmem = pl.BlockSpec(memory_space=pltpu.VMEM)
    far_away = pl.BlockSpec(memory_space=pltpu.HBM)
    return pl.pallas_call(
        functools.partial(tile_kernel, n_core, n_col, side),
        out_shape=(
            jax.ShapeDtypeStruct((kvec, own), jnp.float32),
            jax.ShapeDtypeStruct((n_col - 1, kvec, own), jnp.bfloat16),
            jax.ShapeDtypeStruct((n_col - 1, kvec, own), jnp.float32),
        ),
        in_specs=[pl.BlockSpec(memory_space=pltpu.SMEM)] + [far_away] * 4 + [vmem] * n_core,
        out_specs=(vmem, vmem, vmem),
        scratch_shapes=[
            pltpu.SMEM((slots,), jnp.int32),
            pltpu.SMEM((slots,), jnp.int32),
            pltpu.VMEM((1, own), jnp.float32),
            pltpu.VMEM((slots, area), jnp.bfloat16),
            pltpu.VMEM((n_far * n_core * blk_own + 1, per * kvec, LANES), jnp.float32),
            pltpu.VMEM((n_seg // per * 2 * kvec, per * per * width), jnp.bfloat16),
            pltpu.VMEM((per * per * width, LANES), jnp.bfloat16),
            pltpu.VMEM((n_col, kvec, own), jnp.float32),
            pltpu.SemaphoreType.DMA((slots // CHUNK,)),
            pltpu.SemaphoreType.DMA((3,)),
        ] + [pltpu.VMEM((n_seg, per * kvec, width), jnp.float32)] * SUB,
        compiler_params=pltpu.CompilerParams(vmem_limit_bytes=48 * 2**20),
        cost_estimate=pl.CostEstimate(
            flops=2 * slots * area * kvec, bytes_accessed=2 * slots * area, transcendentals=0
        ),
        name="tile_work",
    )(count, *[pltpu.with_memory_space_constraint(x, pltpu.HBM) for x in (rows, cols, ener, tiles)],
      *gath)


def terms_kernel(own, rest, vec, *refs):
    others, (terms_ref, wide) = refs[:-2], refs[-2:]
    n_col = len(others) + 1
    kvec = vec.shape[0]

    def outer(share, seg):
        return lax.dot_general(
            share, seg[...].astype(jnp.float32), NT,
            precision=lax.Precision.HIGHEST, preferred_element_type=jnp.float32,
        )

    terms = outer(own[...], vec)
    for s in range(1, n_col):
        terms = terms + outer(rest[s - 1], others[n_col - s - 1])
    wide[...] = jnp.zeros(wide.shape, jnp.float32)
    wide[:, :kvec] = terms
    spaced = pltpu.roll(wide[...], 0, 1, stride=kvec, stride_axis=0)
    flat = jnp.sum(spaced, axis=0, keepdims=True)
    for i in range(terms_ref.shape[0]):
        terms_ref[i] = flat


def gram_terms(own, rest, vectors, others, members):
    vmem = pl.BlockSpec(memory_space=pltpu.VMEM)
    return pl.pallas_call(
        terms_kernel,
        out_shape=jax.ShapeDtypeStruct((members, 1, LANES), jnp.float32),
        in_specs=[vmem] * (3 + len(others)),
        out_specs=vmem,
        scratch_shapes=[pltpu.VMEM((vectors.shape[0], LANES), jnp.float32)],
        compiler_params=pltpu.CompilerParams(vmem_limit_bytes=4 * 2**20),
        name="gram_terms",
    )(own, rest, vectors, *others)


def finish_kernel(scale, base, gram_parts, vec, *refs):
    got, (product, residual) = refs[:-2], refs[-2:]
    whole = base[...]
    for piece in got:
        whole = whole + piece[...].astype(jnp.float32)
    product[...] = whole.astype(jnp.bfloat16)
    flat = gram_parts[0]
    for i in range(1, gram_parts.shape[0]):
        flat = flat + gram_parts[i]
    kvec = vec.shape[0]
    lane = lax.broadcasted_iota(jnp.int32, (kvec, LANES), 1)
    first = kvec * lax.broadcasted_iota(jnp.int32, (kvec, LANES), 0)
    wide = jnp.broadcast_to(flat * scale, (kvec, LANES))
    vec32 = vec[...].astype(jnp.float32)
    for a in range(kvec):
        column = jnp.sum(jnp.where(lane == first + a, wide, 0.0), axis=1, keepdims=True)
        whole = whole - column * vec32[a:a + 1, :]
    residual[...] = whole


def finish(scale, base, gram_parts, vectors, got):
    vmem = pl.BlockSpec(memory_space=pltpu.VMEM)
    return pl.pallas_call(
        functools.partial(finish_kernel, scale),
        out_shape=(
            jax.ShapeDtypeStruct(vectors.shape, jnp.bfloat16),
            jax.ShapeDtypeStruct(vectors.shape, jnp.float32),
        ),
        in_specs=[vmem] * (3 + len(got)),
        out_specs=(vmem, vmem),
        compiler_params=pltpu.CompilerParams(vmem_limit_bytes=4 * 2**20),
        name="finish",
    )(base, gram_parts, vectors, *got)


def from_all(x, axis):
    size = lax.axis_size(axis)
    got = [x]
    for s in range(1, size):
        got.append(lax.ppermute(x, axis, [(i, (i + s) % size) for i in range(size)]))
    return got


def per_device(vectors, energies, tiles, tile_rows, tile_cols, tile_count):
    kvec, own = vectors.shape
    n_col = lax.axis_size("col")
    copies = jnp.broadcast_to(vectors[None], (lax.axis_size("far"), kvec, own))
    gath = lax.all_to_all(copies, "far", 0, 0)
    gath = from_all(gath, "core")
    base, send, rest = tile_work(
        tile_rows, tile_cols, tile_count, gath, n_col, energies[None, :], tiles
    )
    got = [
        lax.ppermute(send[s - 1], "col", [(c, (c + s) % n_col) for c in range(n_col)])
        for s in range(1, n_col)
    ]
    others = from_all(vectors, "col")[1:]
    members = lax.axis_size(("far", "core", "col"))
    terms = gram_terms(base, rest, vectors, others, members)
    gram_parts = lax.all_to_all(terms, ("far", "core", "col"), 0, 0)
    return finish(1.0 / (members * own), base, gram_parts, vectors, got)


def solution(mesh):
    n_row, n_col = mesh.devices.shape
    n_core = 2 if n_row % 2 == 0 else 1
    split = ("far", "core", "col")
    chips = Mesh(mesh.devices.reshape(n_row // n_core, n_core, n_col), split)
    in_specs = (P(None, split), P(split), P(split, None), P(split), P(split), P(split))
    out_specs = (P(None, split), P(None, split))
    return jax.shard_map(
        per_device, mesh=chips, in_specs=in_specs, out_specs=out_specs, check_vma=False
    )
```

profile of v0, /device:TPU:0, one launch (start us, length us, event | category | flops | bytes accessed | tf_op | source)
XLA Modules:
  0.0 34.0 jit_solution(6362820355489103927)
XLA Ops:
  0.6 0.0 copy-start
  0.6 0.8 %broadcast_in_dim.10 = bf16[8,8,1024]{2,1,0:T(8,128)(2,1)S(1)} broadcast(bf16[8,1024]{1,0:T(8,128)(2,1)} %vec.3), dimensions={1,2} | broadcast | bytes 147456 | tf_op jit(solution)/shard_map/broadcast_in_dim | solution.py:290
  1.4 14.4 %all_to_all.10.refs_0_ = bf16[8,8,1024]{2,1,0:T(8,128)(2,1)S(1)} all-to-all(bf16[8,8,1024]{2,1,0:T(8,128)(2,1)S(1)} %broadcast_in_dim.10), channel_id=1, replica_groups=mesh['far'=8,'core'=2,'col'=2] {'far'}, dimensions={0} | all-to-all | bytes 262144 | tf_op jit(solution)/shard_map/all_to_all | solution.py:291
  15.8 0.0 collective-permute-start
  15.8 1.5 %collective-permute-start.1 = (bf16[8,1024]{1,0:T(8,128)(2,1)}, bf16[8,1024]{1,0:T(8,128)(2,1)S(1)}, u32[]{:S(2)}, u32[]{:S(2)}) collective-permute-start(bf16[8,1024]{1,0:T(8,128)(2,1)} %vec.3), channel_id=1, source_target_pairs={{0,1},{1,0},{2,3},{3,2},{4,5},{5,4},{6,7},{7,6},{8,9},{9,8},{10,11... | collective-permute-start | bytes 49160 | tf_op jit(solution)/shard_map/ppermute | solution.py:283
  18.0 0.0 collective-permute-done.refs_1_
  18.0 3.0 %tile_work.1 = (f32[8,1024]{1,0:T(8,128)S(1)}, bf16[1,8,1024]{2,1,0:T(8,128)(2,1)S(1)}, f32[1,8,1024]{2,1,0:T(8,128)S(1)}) custom-call(s32[1]{0:T(128)S(6)} %copy.8.count_s, s32[1024]{0:T(1024)} %rows_h.1, s32[1024]{0:T(1024)} %cols_h.1, f32[1,1024]{1,0:T(1,128)} %bitcast.3, bf16[1024,4096]{1,0:T(8,128)(2,1)} %tiles.1, ...), custom_call_target="tpu_custom_call" | custom-call | flops 67108864 | bytes 8388608 | tf_op jit(solution)/shard_map/tile_work/pallas_call | solution.py:179
  21.0 0.0 collective-permute-done.1.refs_0_
  21.0 0.0 copy-done
  21.0 0.9 %gram_terms.1 = f32[32,1,128]{2,1,0:T(1,128)} custom-call(f32[8,1024]{1,0:T(8,128)S(1)} %get-tuple-element.5.own.base, f32[1,8,1024]{2,1,0:T(8,128)S(1)} %get-tuple-element.6.rest, bf16[8,1024]{1,0:T(8,128)(2,1)S(1)} %copy-done, bf16[8,1024]{1,0:T(8,128)(2,1)S(1)} %collective-permute-done.1.refs_0_), custom_call_target="tpu_custom_call" | custom-call | tf_op jit(solution)/shard_map/gram_terms/pallas_call | solution.py:233
  21.9 4.2 %all-to-all-start.1 = ((f32[32,1,128]{2,1,0:T(1,128)}), f32[32,1,128]{2,1,0:T(1,128)S(1)}, u32[]{:S(2)}, u32[]{:S(2)}) async-start(f32[32,1,128]{2,1,0:T(1,128)} %gram_terms.1), calls=%async_computation.1 | async-start | bytes 32768 | tf_op jit(solution)/shard_map/all_to_all | solution.py:303
  26.1 1.8 %collective-permute-start.2 = (bf16[8,1024]{1,0:T(8,128)(2,1)S(1)}, bf16[8,1024]{1,0:T(8,128)(2,1)S(1)}, u32[]{:S(2)}, u32[]{:S(2)}) collective-permute-start(bf16[8,1024]{1,0:T(8,128)(2,1)S(1)} %bitcast.2), channel_id=1, source_target_pairs={{0,1},{1,0},{2,3},{3,2},{4,5},{5,4},{6,7},{7,6},{8,9},{9,8},{10,11... | collective-permute-start | bytes 49160 | tf_op jit(solution)/shard_map/ppermute | solution.py:297
  27.9 2.0 %collective-permute-done.2.refs_0_ = bf16[8,1024]{1,0:T(8,128)(2,1)S(1)} collective-permute-done((bf16[8,1024]{1,0:T(8,128)(2,1)S(1)}, bf16[8,1024]{1,0:T(8,128)(2,1)S(1)}, u32[]{:S(2)}, u32[]{:S(2)}) %collective-permute-start.2) | collective-permute-done | bytes 16416 | tf_op jit(solution)/shard_map/ppermute | solution.py:297
  29.9 3.3 %all-to-all-done.1.gram_parts = f32[32,1,128]{2,1,0:T(1,128)S(1)} async-done(((f32[32,1,128]{2,1,0:T(1,128)}), f32[32,1,128]{2,1,0:T(1,128)S(1)}, u32[]{:S(2)}, u32[]{:S(2)}) %all-to-all-start.1) | async-done | bytes 16416 | tf_op jit(solution)/shard_map/all_to_all | solution.py:303
  33.2 0.8 %finish.1 = (bf16[8,1024]{1,0:T(8,128)(2,1)}, f32[8,1024]{1,0:T(8,128)}) custom-call(f32[8,1024]{1,0:T(8,128)S(1)} %get-tuple-element.5.own.base, f32[32,1,128]{2,1,0:T(1,128)S(1)} %all-to-all-done.1.gram_parts, bf16[8,1024]{1,0:T(8,128)(2,1)S(1)} %copy-done, bf16[8,1024]{1,0:T(8,128)(2,1)S(1)} %collective-permute-done.2.refs_0_), custom_call_target="tpu_custom_call" | custom-call | tf_op jit(solution)/shard_map/finish/pallas_call | solution.py:266
Async XLA Ops:
  0.6 20.4 %copy-start = (bf16[8,1024]{1,0:T(8,128)(2,1)S(1)}, bf16[8,1024]{1,0:T(8,128)(2,1)}, u32[]{:S(2)}) copy-start(bf16[8,1024]{1,0:T(8,128)(2,1)} %vec.3) | copy-start | bytes 49156
  15.8 2.2 %collective-permute-start = (bf16[8,8,1024]{2,1,0:T(8,128)(2,1)S(1)}, bf16[8,8,1024]{2,1,0:T(8,128)(2,1)S(1)}, u32[]{:S(2)}, u32[]{:S(2)}) collective-permute-start(bf16[8,8,1024]{2,1,0:T(8,128)(2,1)S(1)} %all_to_all.10.refs_0_), channel_id=1, source_target_pairs={{0,2},{2,0},{1,3},{3,1},{4,6},{6,4},{5,7},{7,5},{8,10},{10,8},{9,1... | collective-permute-start | bytes 393224 | tf_op jit(solution)/shard_map/ppermute | solution.py:283
  15.8 5.1 %collective-permute-start.1 = (bf16[8,1024]{1,0:T(8,128)(2,1)}, bf16[8,1024]{1,0:T(8,128)(2,1)S(1)}, u32[]{:S(2)}, u32[]{:S(2)}) collective-permute-start(bf16[8,1024]{1,0:T(8,128)(2,1)} %vec.3), channel_id=1, source_target_pairs={{0,1},{1,0},{2,3},{3,2},{4,5},{5,4},{6,7},{7,6},{8,9},{9,8},{10,11... | collective-permute-start | bytes 49160 | tf_op jit(solution)/shard_map/ppermute | solution.py:283
  21.9 11.3 %all-to-all-start.1 = ((f32[32,1,128]{2,1,0:T(1,128)}), f32[32,1,128]{2,1,0:T(1,128)S(1)}, u32[]{:S(2)}, u32[]{:S(2)}) async-start(f32[32,1,128]{2,1,0:T(1,128)} %gram_terms.1), calls=%async_computation.1 | async-start | bytes 32768 | tf_op jit(solution)/shard_map/all_to_all | solution.py:303
  26.1 3.8 %collective-permute-start.2 = (bf16[8,1024]{1,0:T(8,128)(2,1)S(1)}, bf16[8,1024]{1,0:T(8,128)(2,1)S(1)}, u32[]{:S(2)}, u32[]{:S(2)}) collective-permute-start(bf16[8,1024]{1,0:T(8,128)(2,1)S(1)} %bitcast.2), channel_id=1, source_target_pairs={{0,1},{1,0},{2,3},{3,2},{4,5},{5,4},{6,7},{7,6},{8,9},{9,8},{10,11... | collective-permute-start | bytes 49160 | tf_op jit(solution)/shard_map/ppermute | solution.py:297
where the time goes:
time: 34.1 us; the launch traced here: 34 us
  blocking collectives  14.4 us (42%)
  starting transfers between devices  7.52 us (22%)
  waiting for transfers between devices  5.29 us (16%)
  Pallas kernels  4.63 us (14%)
  between operations  1.33 us (4%)
  local copies, waits for them, and re-layouts  0.8 us (2%)
    all_to_all x1, blocking collectives, per_device(): gath = lax.all_to_all(copies, 'far', 0, 0)  14.4 us
    all_to_all x1, starting transfers between devices, per_device(): gram_parts = lax.all_to_all(terms, ('far', 'core', 'col'), 0, 0)  4.16 us
    all_to_all x1, waiting for transfers between devices, per_device(): gram_parts = lax.all_to_all(terms, ('far', 'core', 'col'), 0, 0)  3.3 us
    pallas_call x1, Pallas kernels, tile_work(): pl.pallas_call(functools.partial(tile_kernel, n_core, n_col, side), out_s...  2.95 us
    ppermute x1, waiting for transfers between devices, per_device(): lax.ppermute(send[s - 1], 'col', [(c, (c + s) % n_col) for c in range(n_c...  1.99 us
    ppermute x1, starting transfers between devices, per_device(): lax.ppermute(send[s - 1], 'col', [(c, (c + s) % n_col) for c in range(n_c...  1.83 us
    ppermute x2, starting transfers between devices, from_all(): lax.ppermute(x, axis, [(i, (i + s) % size) for i in range(size)])  1.52 us
    pallas_call x1, Pallas kernels, gram_terms(): pl.pallas_call(terms_kernel, out_shape=jax.ShapeDtypeStruct((members, 1,...  0.92 us
  transfers between devices with their start and end apart: 4, of which 2 were waited for; matrix products, arithmetic and copies ran while one was open for 0% of the time, Pallas kernels for 9%

commit v1 on v0

--- a/solution.py
+++ b/solution.py
@@ -223,16 +223,14 @@
     wide[...] = jnp.zeros(wide.shape, jnp.float32)
     wide[:, :kvec] = terms
     spaced = pltpu.roll(wide[...], 0, 1, stride=kvec, stride_axis=0)
-    flat = jnp.sum(spaced, axis=0, keepdims=True)
-    for i in range(terms_ref.shape[0]):
-        terms_ref[i] = flat
-
-
-def gram_terms(own, rest, vectors, others, members):
+    terms_ref[...] = jnp.sum(spaced, axis=0, keepdims=True)
+
+
+def gram_terms(own, rest, vectors, others):
     vmem = pl.BlockSpec(memory_space=pltpu.VMEM)
     return pl.pallas_call(
         terms_kernel,
-        out_shape=jax.ShapeDtypeStruct((members, 1, LANES), jnp.float32),
+        out_shape=jax.ShapeDtypeStruct((1, LANES), jnp.float32),
         in_specs=[vmem] * (3 + len(others)),
         out_specs=vmem,
         scratch_shapes=[pltpu.VMEM((vectors.shape[0], LANES), jnp.float32)],
@@ -298,10 +296,12 @@
         for s in range(1, n_col)
     ]
     others = from_all(vectors, "col")[1:]
-    members = lax.axis_size(("far", "core", "col"))
-    terms = gram_terms(base, rest, vectors, others, members)
-    gram_parts = lax.all_to_all(terms, ("far", "core", "col"), 0, 0)
-    return finish(1.0 / (members * own), base, gram_parts, vectors, got)
+    terms = sum(from_all(gram_terms(base, rest, vectors, others), "core"))
+    members = lax.axis_size(("far", "col"))
+    terms = jnp.broadcast_to(terms[None], (members,) + terms.shape)
+    gram_parts = lax.all_to_all(terms, ("far", "col"), 0, 0)
+    states = lax.axis_size(("far", "core", "col")) * own
+    return finish(1.0 / states, base, gram_parts, vectors, got)
 
 
 def solution(mesh):

time: 34.1 us -> 36 us (1.056); the launches traced: 34 us -> 35.5 us
  blocking collectives: 14.4 us -> 24.4 us
  waiting for transfers between devices: 5.29 us -> 0.01 us
  starting transfers between devices: 7.52 us -> 4.46 us
    all_to_all x0 -> x1, blocking collectives: none -> 9.99 us  [per_device(): gram_parts = lax.all_to_all(terms, ('far', 'col'), 0, 0)]
    all_to_all x1 -> x0, starting transfers between devices: 4.16 us -> none  [per_device(): gram_parts = lax.all_to_all(terms, ('far', 'core', 'col'), 0, 0)]
    all_to_all x1 -> x0, waiting for transfers between devices: 3.3 us -> none  [per_device(): gram_parts = lax.all_to_all(terms, ('far', 'core', 'col'), 0, 0)]
    ppermute x1, waiting for transfers between devices: 1.99 us -> 0.01 us  [per_device(): lax.ppermute(send[s - 1], 'col', [(c, (c + s) % n_col) for c in range(n_c...]
    ppermute x2 -> x3, starting transfers between devices: 1.52 us -> 2.23 us  [from_all(): lax.ppermute(x, axis, [(i, (i + s) % size) for i in range(size)])]
    pallas_call x1, Pallas kernels: 0.92 us -> 0.31 us  [gram_terms(): pl.pallas_call(terms_kernel, out_shape=jax.ShapeDtypeStruct((1, LANES), j...]
    pallas_call x1, Pallas kernels: 2.95 us -> 3.42 us  [tile_work(): pl.pallas_call(functools.partial(tile_kernel, n_core, n_col, side), out_s...]
    ppermute x1, starting transfers between devices: 1.83 us -> 2.23 us  [per_device(): lax.ppermute(send[s - 1], 'col', [(c, (c + s) % n_col) for c in range(n_c...]
  transfers between devices with their start and end apart: 4 -> 4, of which waited for: 2 -> 0; matrix products, arithmetic and copies ran while one was open for 0% -> 0% of each run, Pallas kernels for 9% -> 10%
where the time goes in v1:
time: 36 us; the launch traced here: 35.5 us
  blocking collectives  24.4 us (68%)
  Pallas kernels  4.47 us (12%)
  starting transfers between devices  4.46 us (12%)
  between operations  1.33 us (4%)
  local copies, waits for them, and re-layouts  0.81 us (2%)
    all_to_all x1, blocking collectives, per_device(): gath = lax.all_to_all(copies, 'far', 0, 0)  14.4 us
    all_to_all x1, blocking collectives, per_device(): gram_parts = lax.all_to_all(terms, ('far', 'col'), 0, 0)  9.99 us
    pallas_call x1, Pallas kernels, tile_work(): pl.pallas_call(functools.partial(tile_kernel, n_core, n_col, side), out_s...  3.42 us
    ppermute x1, starting transfers between devices, per_device(): lax.ppermute(send[s - 1], 'col', [(c, (c + s) % n_col) for c in range(n_c...  2.23 us
    ppermute x3, starting transfers between devices, from_all(): lax.ppermute(x, axis, [(i, (i + s) % size) for i in range(size)])  2.23 us
    broadcast_in_dim x1, local copies, waits for them, and re-layouts, per_device(): copies = jnp.broadcast_to(vectors[None], (lax.axis_size('far'), kvec, own))  0.79 us
    pallas_call x1, Pallas kernels, finish(): pl.pallas_call(functools.partial(finish_kernel, scale), out_shape=(jax.Sh...  0.74 us
  transfers between devices with their start and end apart: 4, of which 0 were waited for; matrix products, arithmetic and copies ran while one was open for 0% of the time, Pallas kernels for 10%

profile of v1, /device:TPU:0, one launch (start us, length us, event | category | flops | bytes accessed | tf_op | source)
XLA Modules:
  0.0 35.5 jit_solution(11123512701492768296)
XLA Ops:
  0.6 0.0 copy-start
  0.6 0.8 %broadcast_in_dim.18 = bf16[8,8,1024]{2,1,0:T(8,128)(2,1)S(1)} broadcast(bf16[8,1024]{1,0:T(8,128)(2,1)} %vec.3), dimensions={1,2} | broadcast | bytes 147456 | tf_op jit(solution)/shard_map/broadcast_in_dim | solution.py:288
  1.4 14.4 %all_to_all.10.refs_0_ = bf16[8,8,1024]{2,1,0:T(8,128)(2,1)S(1)} all-to-all(bf16[8,8,1024]{2,1,0:T(8,128)(2,1)S(1)} %broadcast_in_dim.18), channel_id=1, replica_groups=mesh['far'=8,'core'=2,'col'=2] {'far'}, dimensions={0} | all-to-all | bytes 262144 | tf_op jit(solution)/shard_map/all_to_all | solution.py:289
  15.8 0.0 collective-permute-start
  15.8 1.5 %collective-permute-start.1 = (bf16[8,1024]{1,0:T(8,128)(2,1)}, bf16[8,1024]{1,0:T(8,128)(2,1)S(1)}, u32[]{:S(2)}, u32[]{:S(2)}) collective-permute-start(bf16[8,1024]{1,0:T(8,128)(2,1)} %vec.3), channel_id=1, source_target_pairs={{0,1},{1,0},{2,3},{3,2},{4,5},{5,4},{6,7},{7,6},{8,9},{9,8},{10,11... | collective-permute-start | bytes 49160 | tf_op jit(solution)/shard_map/ppermute | solution.py:281
  18.0 0.0 collective-permute-done.refs_1_
  18.0 3.4 %tile_work.1 = (f32[8,1024]{1,0:T(8,128)S(1)}, bf16[1,8,1024]{2,1,0:T(8,128)(2,1)S(1)}, f32[1,8,1024]{2,1,0:T(8,128)S(1)}) custom-call(s32[1]{0:T(128)S(6)} %copy.8.count_s, s32[1024]{0:T(1024)} %rows_h.1, s32[1024]{0:T(1024)} %cols_h.1, f32[1,1024]{1,0:T(1,128)} %bitcast.5, bf16[1024,4096]{1,0:T(8,128)(2,1)} %tiles.1, ...), custom_call_target="tpu_custom_call" | custom-call | flops 67108864 | bytes 8388608 | tf_op jit(solution)/shard_map/tile_work/pallas_call | solution.py:179
  21.4 0.0 collective-permute-done.1.refs_0_
  21.4 0.0 copy-done
  21.5 0.3 gram_terms.1
  21.8 0.7 %collective-permute-start.2 = (f32[1,128]{1,0:T(1,128)S(1)}, f32[1,128]{1,0:T(1,128)S(1)}, u32[]{:S(2)}, u32[]{:S(2)}) collective-permute-start(f32[1,128]{1,0:T(1,128)S(1)} %gram_terms.1), channel_id=1, source_target_pairs={{0,2},{2,0},{1,3},{3,1},{4,6},{6,4},{5,7},{7,5},{8,10},{10,8},{9,1... | collective-permute-start | bytes 1544 | tf_op jit(solution)/shard_map/ppermute | solution.py:281
  22.5 2.2 %collective-permute-start.3 = (bf16[8,1024]{1,0:T(8,128)(2,1)S(1)}, bf16[8,1024]{1,0:T(8,128)(2,1)S(1)}, u32[]{:S(2)}, u32[]{:S(2)}) collective-permute-start(bf16[8,1024]{1,0:T(8,128)(2,1)S(1)} %bitcast.4), channel_id=1, source_target_pairs={{0,1},{1,0},{2,3},{3,2},{4,5},{5,4},{6,7},{7,6},{8,9},{9,8},{10,11... | collective-permute-start | bytes 49160 | tf_op jit(solution)/shard_map/ppermute | solution.py:295
  24.7 0.0 collective-permute-done.2
  24.7 10.0 %all_to_all.11.gram_parts = f32[16,1,128]{2,1,0:T(1,128)S(1)} all-to-all(f32[16,1,128]{2,1,0:T(1,128)S(1)} %broadcast_in_dim.20), channel_id=1, replica_groups=mesh['far'=8,'core'=2,'col'=2] {'far','col'}, dimensions={0} | all-to-all | bytes 16384 | tf_op jit(solution)/shard_map/all_to_all | solution.py:302
  34.7 0.0 collective-permute-done.3.refs_0_
  34.7 0.7 %finish.1 = (bf16[8,1024]{1,0:T(8,128)(2,1)}, f32[8,1024]{1,0:T(8,128)}) custom-call(f32[8,1024]{1,0:T(8,128)S(1)} %get-tuple-element.5.own.base, f32[16,1,128]{2,1,0:T(1,128)S(1)} %all_to_all.11.gram_parts, bf16[8,1024]{1,0:T(8,128)(2,1)S(1)} %copy-done, bf16[8,1024]{1,0:T(8,128)(2,1)S(1)} %collective-permute-done.3.refs_0_), custom_call_target="tpu_custom_call" | custom-call | tf_op jit(solution)/shard_map/finish/pallas_call | solution.py:264
  (2 shorter events, 0.0 us)
Async XLA Ops:
  0.6 20.8 %copy-start = (bf16[8,1024]{1,0:T(8,128)(2,1)S(1)}, bf16[8,1024]{1,0:T(8,128)(2,1)}, u32[]{:S(2)}) copy-start(bf16[8,1024]{1,0:T(8,128)(2,1)} %vec.3) | copy-start | bytes 49156
  15.8 2.2 %collective-permute-start = (bf16[8,8,1024]{2,1,0:T(8,128)(2,1)S(1)}, bf16[8,8,1024]{2,1,0:T(8,128)(2,1)S(1)}, u32[]{:S(2)}, u32[]{:S(2)}) collective-permute-start(bf16[8,8,1024]{2,1,0:T(8,128)(2,1)S(1)} %all_to_all.10.refs_0_), channel_id=1, source_target_pairs={{0,2},{2,0},{1,3},{3,1},{4,6},{6,4},{5,7},{7,5},{8,10},{10,8},{9,1... | collective-permute-start | bytes 393224 | tf_op jit(solution)/shard_map/ppermute | solution.py:281
  15.8 5.6 %collective-permute-start.1 = (bf16[8,1024]{1,0:T(8,128)(2,1)}, bf16[8,1024]{1,0:T(8,128)(2,1)S(1)}, u32[]{:S(2)}, u32[]{:S(2)}) collective-permute-start(bf16[8,1024]{1,0:T(8,128)(2,1)} %vec.3), channel_id=1, source_target_pairs={{0,1},{1,0},{2,3},{3,2},{4,5},{5,4},{6,7},{7,6},{8,9},{9,8},{10,11... | collective-permute-start | bytes 49160 | tf_op jit(solution)/shard_map/ppermute | solution.py:281
  21.8 2.9 %collective-permute-start.2 = (f32[1,128]{1,0:T(1,128)S(1)}, f32[1,128]{1,0:T(1,128)S(1)}, u32[]{:S(2)}, u32[]{:S(2)}) collective-permute-start(f32[1,128]{1,0:T(1,128)S(1)} %gram_terms.1), channel_id=1, source_target_pairs={{0,2},{2,0},{1,3},{3,1},{4,6},{6,4},{5,7},{7,5},{8,10},{10,8},{9,1... | collective-permute-start | bytes 1544 | tf_op jit(solution)/shard_map/ppermute | solution.py:281
  22.5 12.2 %collective-permute-start.3 = (bf16[8,1024]{1,0:T(8,128)(2,1)S(1)}, bf16[8,1024]{1,0:T(8,128)(2,1)S(1)}, u32[]{:S(2)}, u32[]{:S(2)}) collective-permute-start(bf16[8,1024]{1,0:T(8,128)(2,1)S(1)} %bitcast.4), channel_id=1, source_target_pairs={{0,1},{1,0},{2,3},{3,2},{4,5},{5,4},{6,7},{7,6},{8,9},{9,8},{10,11... | collective-permute-start | bytes 49160 | tf_op jit(solution)/shard_map/ppermute | solution.py:295

commit v2 on v1

--- a/solution.py
+++ b/solution.py
@@ -11,6 +11,8 @@
 LANES = 128
 SUB = 8
 CHUNK = 128
+STEP = 256
+SUMS = 4
 
 NT = (((1,), (1,)), ((), ()))
 
@@ -104,16 +106,20 @@
         left = jnp.concatenate(entries, axis=0).astype(jnp.bfloat16)
         return lax.dot_general(left, w, NT, preferred_element_type=jnp.float32)
 
+    lane_w = lax.broadcasted_iota(jnp.int32, (rows_of, width), 1) % SUB
+
     def accumulate(at, out):
         for t in range(SUB):
             r = rows_s[at + t]
-            acc[t][r] += out[t * rows_of:(t + 1) * rows_of]
-
-    def one_chunk(ch, check):
-        tile_copy(ch).wait()
+            mine = jnp.where(lane_w == t, out[t * rows_of:(t + 1) * rows_of], 0.0)
+            acc[t % len(acc)][r] += mine
+
+    def step(first, slots_in, check):
+        for i in range(slots_in // CHUNK):
+            tile_copy(first // CHUNK + i).wait()
         waiting = None
-        for q in range(CHUNK // (2 * SUB)):
-            base = pl.multiple_of(ch * CHUNK + q * 2 * SUB, 2 * SUB)
+        for q in range(slots_in // (2 * SUB)):
+            base = pl.multiple_of(first + q * 2 * SUB, 2 * SUB)
             x = buf[pl.ds(base, 2 * SUB), :].astype(jnp.float32)
             for half in range(2):
                 out = product(base, half, x, check)
@@ -122,25 +128,26 @@
                 waiting = (base + half * SUB, out)
         accumulate(*waiting)
 
-    def full_chunk(ch, carry):
-        one_chunk(ch, False)
-        return carry
-
-    lax.fori_loop(0, count // CHUNK, full_chunk, 0)
-
-    @pl.when(used > count // CHUNK)
-    def _():
-        one_chunk(used - 1, True)
-
-    lane_w = lax.broadcasted_iota(jnp.int32, (rows_of, width), 1) % SUB
+    def full_step(i, carry):
+        step(i * STEP, STEP, False)
+        return carry
+
+    def last_step(ch, carry):
+        step(ch * CHUNK, CHUNK, True)
+        return carry
+
+    full = count // STEP
+    lax.fori_loop(0, full, full_step, 0)
+    lax.fori_loop(full * (STEP // CHUNK), used, last_step, 0)
+
     pairs = n_seg // per
 
     def pick(m, carry):
         pieces = []
         for par in range(per):
-            total = jnp.zeros((rows_of, width), jnp.float32)
-            for t in range(SUB):
-                total = jnp.where(lane_w == t, acc[t][m * per + par], total)
+            total = acc[0][m * per + par]
+            for other in acc[1:]:
+                total = total + other[m * per + par]
             for jp in range(per):
                 pieces.append(total[jp * kvec:(jp + 1) * kvec])
         a = jnp.concatenate(pieces, axis=1)
@@ -196,7 +203,7 @@
             pltpu.VMEM((n_col, kvec, own), jnp.float32),
             pltpu.SemaphoreType.DMA((slots // CHUNK,)),
             pltpu.SemaphoreType.DMA((3,)),
-        ] + [pltpu.VMEM((n_seg, per * kvec, width), jnp.float32)] * SUB,
+        ] + [pltpu.VMEM((n_seg, per * kvec, width), jnp.float32)] * SUMS,
         compiler_params=pltpu.CompilerParams(vmem_limit_bytes=48 * 2**20),
         cost_estimate=pl.CostEstimate(
             flops=2 * slots * area * kvec, bytes_accessed=2 * slots * area, transcendentals=0
@@ -296,12 +303,11 @@
         for s in range(1, n_col)
     ]
     others = from_all(vectors, "col")[1:]
-    terms = sum(from_all(gram_terms(base, rest, vectors, others), "core"))
-    members = lax.axis_size(("far", "col"))
+    members = lax.axis_size(("far", "core", "col"))
+    terms = gram_terms(base, rest, vectors, others)
     terms = jnp.broadcast_to(terms[None], (members,) + terms.shape)
-    gram_parts = lax.all_to_all(terms, ("far", "col"), 0, 0)
-    states = lax.axis_size(("far", "core", "col")) * own
-    return finish(1.0 / states, base, gram_parts, vectors, got)
+    gram_parts = lax.all_to_all(terms, ("far", "core", "col"), 0, 0)
+    return finish(1.0 / (members * own), base, gram_parts, vectors, got)
 
 
 def solution(mesh):

time: 36 us -> 34 us (0.944)
  blocking collectives: 24.4 us -> 14.4 us
  waiting for transfers between devices: 0.01 us -> 5.41 us
  starting transfers between devices: 4.46 us -> 5.78 us
  Pallas kernels: 4.47 us -> 5.2 us
  local copies, waits for them, and re-layouts: 0.81 us -> 1.43 us
    all_to_all x1 -> x0, blocking collectives: 9.99 us -> none  [per_device(): gram_parts = lax.all_to_all(terms, ('far', 'col'), 0, 0)]
    all_to_all x0 -> x1, waiting for transfers between devices: none -> 3.31 us  [per_device(): gram_parts = lax.all_to_all(terms, ('far', 'core', 'col'), 0, 0)]
    all_to_all x0 -> x1, starting transfers between devices: none -> 2.54 us  [per_device(): gram_parts = lax.all_to_all(terms, ('far', 'core', 'col'), 0, 0)]
    ppermute x1, waiting for transfers between devices: 0.01 us -> 2.1 us  [per_device(): lax.ppermute(send[s - 1], 'col', [(c, (c + s) % n_col) for c in range(n_c...]
    pallas_call x1, Pallas kernels: 3.42 us -> 4.13 us  [tile_work(): pl.pallas_call(functools.partial(tile_kernel, n_core, n_col, side), out_s...]
    ppermute x3 -> x2, starting transfers between devices: 2.23 us -> 1.52 us  [from_all(): lax.ppermute(x, axis, [(i, (i + s) % size) for i in range(size)])]
    broadcast_in_dim x1, local copies, waits for them, and re-layouts: 0.01 us -> 0.63 us  [per_device(): terms = jnp.broadcast_to(terms[None], (members,) + terms.shape)]
    ppermute x1, starting transfers between devices: 2.23 us -> 1.72 us  [per_device(): lax.ppermute(send[s - 1], 'col', [(c, (c + s) % n_col) for c in range(n_c...]
  transfers between devices with their start and end apart: 4 -> 4, of which waited for: 0 -> 2; matrix products, arithmetic and copies ran while one was open for 0% -> 0% of each run, Pallas kernels for 10% -> 12%
where the time goes in v2:
time: 34 us; the launch traced here: 33.5 us
  blocking collectives  14.4 us (42%)
  starting transfers between devices  5.78 us (17%)
  waiting for transfers between devices  5.41 us (16%)
  Pallas kernels  5.2 us (15%)
  local copies, waits for them, and re-layouts  1.43 us (4%)
  between operations  1.33 us (4%)
    all_to_all x1, blocking collectives, per_device(): gath = lax.all_to_all(copies, 'far', 0, 0)  14.4 us
    pallas_call x1, Pallas kernels, tile_work(): pl.pallas_call(functools.partial(tile_kernel, n_core, n_col, side), out_s...  4.13 us
    all_to_all x1, waiting for transfers between devices, per_device(): gram_parts = lax.all_to_all(terms, ('far', 'core', 'col'), 0, 0)  3.31 us
    all_to_all x1, starting transfers between devices, per_device(): gram_parts = lax.all_to_all(terms, ('far', 'core', 'col'), 0, 0)  2.54 us
    ppermute x1, waiting for transfers between devices, per_device(): lax.ppermute(send[s - 1], 'col', [(c, (c + s) % n_col) for c in range(n_c...  2.1 us
    ppermute x1, starting transfers between devices, per_device(): lax.ppermute(send[s - 1], 'col', [(c, (c + s) % n_col) for c in range(n_c...  1.72 us
    ppermute x2, starting transfers between devices, from_all(): lax.ppermute(x, axis, [(i, (i + s) % size) for i in range(size)])  1.52 us
    broadcast_in_dim x1, local copies, waits for them, and re-layouts, per_device(): copies = jnp.broadcast_to(vectors[None], (lax.axis_size('far'), kvec, own))  0.79 us
  transfers between devices with their start and end apart: 4, of which 2 were waited for; matrix products, arithmetic and copies ran while one was open for 0% of the time, Pallas kernels for 12%

profile of v2, /device:TPU:0, one launch (start us, length us, event | category | flops | bytes accessed | tf_op | source)
XLA Modules:
  0.0 33.5 jit_solution(3653287219124610086)
XLA Ops:
  0.6 0.0 copy-start
  0.6 0.8 %broadcast_in_dim.18 = bf16[8,8,1024]{2,1,0:T(8,128)(2,1)S(1)} broadcast(bf16[8,1024]{1,0:T(8,128)(2,1)} %vec.3), dimensions={1,2} | broadcast | bytes 147456 | tf_op jit(solution)/shard_map/broadcast_in_dim | solution.py:295
  1.4 14.4 %all_to_all.10.refs_0_ = bf16[8,8,1024]{2,1,0:T(8,128)(2,1)S(1)} all-to-all(bf16[8,8,1024]{2,1,0:T(8,128)(2,1)S(1)} %broadcast_in_dim.18), channel_id=1, replica_groups=mesh['far'=8,'core'=2,'col'=2] {'far'}, dimensions={0} | all-to-all | bytes 262144 | tf_op jit(solution)/shard_map/all_to_all | solution.py:296
  15.8 0.0 collective-permute-start
  15.8 1.5 %collective-permute-start.1 = (bf16[8,1024]{1,0:T(8,128)(2,1)}, bf16[8,1024]{1,0:T(8,128)(2,1)S(1)}, u32[]{:S(2)}, u32[]{:S(2)}) collective-permute-start(bf16[8,1024]{1,0:T(8,128)(2,1)} %vec.3), channel_id=1, source_target_pairs={{0,1},{1,0},{2,3},{3,2},{4,5},{5,4},{6,7},{7,6},{8,9},{9,8},{10,11... | collective-permute-start | bytes 49160 | tf_op jit(solution)/shard_map/ppermute | solution.py:288
  18.0 0.0 collective-permute-done.refs_1_
  18.0 4.1 %tile_work.1 = (f32[8,1024]{1,0:T(8,128)S(1)}, bf16[1,8,1024]{2,1,0:T(8,128)(2,1)S(1)}, f32[1,8,1024]{2,1,0:T(8,128)S(1)}) custom-call(s32[1]{0:T(128)S(6)} %copy.8.count_s, s32[1024]{0:T(1024)} %rows_h.1, s32[1024]{0:T(1024)} %cols_h.1, f32[1,1024]{1,0:T(1,128)} %bitcast.5, bf16[1024,4096]{1,0:T(8,128)(2,1)} %tiles.1, ...), custom_call_target="tpu_custom_call" | custom-call | flops 67108864 | bytes 8388608 | tf_op jit(solution)/shard_map/tile_work/pallas_call | solution.py:186
  22.2 0.0 collective-permute-done.1.refs_0_
  22.2 0.0 copy-done
  22.2 0.3 gram_terms.1
  22.5 0.6 %broadcast_in_dim.20 = f32[32,1,128]{2,1,0:T(1,128)} broadcast(f32[128]{0:T(128)S(1)} %bitcast.3), dimensions={2} | broadcast | bytes 16896 | tf_op jit(solution)/shard_map/broadcast_in_dim | solution.py:308
  23.1 2.5 %all-to-all-start.1 = ((f32[32,1,128]{2,1,0:T(1,128)}), f32[32,1,128]{2,1,0:T(1,128)S(1)}, u32[]{:S(2)}, u32[]{:S(2)}) async-start(f32[32,1,128]{2,1,0:T(1,128)} %broadcast_in_dim.20), calls=%async_computation.1 | async-start | bytes 32768 | tf_op jit(solution)/shard_map/all_to_all | solution.py:309
  25.7 1.7 %collective-permute-start.2 = (bf16[8,1024]{1,0:T(8,128)(2,1)S(1)}, bf16[8,1024]{1,0:T(8,128)(2,1)S(1)}, u32[]{:S(2)}, u32[]{:S(2)}) collective-permute-start(bf16[8,1024]{1,0:T(8,128)(2,1)S(1)} %bitcast.4), channel_id=1, source_target_pairs={{0,1},{1,0},{2,3},{3,2},{4,5},{5,4},{6,7},{7,6},{8,9},{9,8},{10,11... | collective-permute-start | bytes 49160 | tf_op jit(solution)/shard_map/ppermute | solution.py:302
  27.4 2.1 %collective-permute-done.2.refs_0_ = bf16[8,1024]{1,0:T(8,128)(2,1)S(1)} collective-permute-done((bf16[8,1024]{1,0:T(8,128)(2,1)S(1)}, bf16[8,1024]{1,0:T(8,128)(2,1)S(1)}, u32[]{:S(2)}, u32[]{:S(2)}) %collective-permute-start.2) | collective-permute-done | bytes 16416 | tf_op jit(solution)/shard_map/ppermute | solution.py:302
  29.5 3.3 %all-to-all-done.1.gram_parts = f32[32,1,128]{2,1,0:T(1,128)S(1)} async-done(((f32[32,1,128]{2,1,0:T(1,128)}), f32[32,1,128]{2,1,0:T(1,128)S(1)}, u32[]{:S(2)}, u32[]{:S(2)}) %all-to-all-start.1) | async-done | bytes 16416 | tf_op jit(solution)/shard_map/all_to_all | solution.py:309
  32.8 0.8 %finish.1 = (bf16[8,1024]{1,0:T(8,128)(2,1)}, f32[8,1024]{1,0:T(8,128)}) custom-call(f32[8,1024]{1,0:T(8,128)S(1)} %get-tuple-element.5.own.base, f32[32,1,128]{2,1,0:T(1,128)S(1)} %all-to-all-done.1.gram_parts, bf16[8,1024]{1,0:T(8,128)(2,1)S(1)} %copy-done, bf16[8,1024]{1,0:T(8,128)(2,1)S(1)} %collective-permute-done.2.refs_0_), custom_call_target="tpu_custom_call" | custom-call | tf_op jit(solution)/shard_map/finish/pallas_call | solution.py:271
Async XLA Ops:
  0.6 21.5 %copy-start = (bf16[8,1024]{1,0:T(8,128)(2,1)S(1)}, bf16[8,1024]{1,0:T(8,128)(2,1)}, u32[]{:S(2)}) copy-start(bf16[8,1024]{1,0:T(8,128)(2,1)} %vec.3) | copy-start | bytes 49156
  15.8 2.2 %collective-permute-start = (bf16[8,8,1024]{2,1,0:T(8,128)(2,1)S(1)}, bf16[8,8,1024]{2,1,0:T(8,128)(2,1)S(1)}, u32[]{:S(2)}, u32[]{:S(2)}) collective-permute-start(bf16[8,8,1024]{2,1,0:T(8,128)(2,1)S(1)} %all_to_all.10.refs_0_), channel_id=1, source_target_pairs={{0,2},{2,0},{1,3},{3,1},{4,6},{6,4},{5,7},{7,5},{8,10},{10,8},{9,1... | collective-permute-start | bytes 393224 | tf_op jit(solution)/shard_map/ppermute | solution.py:288
  15.8 6.3 %collective-permute-start.1 = (bf16[8,1024]{1,0:T(8,128)(2,1)}, bf16[8,1024]{1,0:T(8,128)(2,1)S(1)}, u32[]{:S(2)}, u32[]{:S(2)}) collective-permute-start(bf16[8,1024]{1,0:T(8,128)(2,1)} %vec.3), channel_id=1, source_target_pairs={{0,1},{1,0},{2,3},{3,2},{4,5},{5,4},{6,7},{7,6},{8,9},{9,8},{10,11... | collective-permute-start | bytes 49160 | tf_op jit(solution)/shard_map/ppermute | solution.py:288
  23.1 9.7 %all-to-all-start.1 = ((f32[32,1,128]{2,1,0:T(1,128)}), f32[32,1,128]{2,1,0:T(1,128)S(1)}, u32[]{:S(2)}, u32[]{:S(2)}) async-start(f32[32,1,128]{2,1,0:T(1,128)} %broadcast_in_dim.20), calls=%async_computation.1 | async-start | bytes 32768 | tf_op jit(solution)/shard_map/all_to_all | solution.py:309
  25.7 3.8 %collective-permute-start.2 = (bf16[8,1024]{1,0:T(8,128)(2,1)S(1)}, bf16[8,1024]{1,0:T(8,128)(2,1)S(1)}, u32[]{:S(2)}, u32[]{:S(2)}) collective-permute-start(bf16[8,1024]{1,0:T(8,128)(2,1)S(1)} %bitcast.4), channel_id=1, source_target_pairs={{0,1},{1,0},{2,3},{3,2},{4,5},{5,4},{6,7},{7,6},{8,9},{9,8},{10,11... | collective-permute-start | bytes 49160 | tf_op jit(solution)/shard_map/ppermute | solution.py:302

commit v3 on v2

--- a/solution.py
+++ b/solution.py
@@ -18,22 +18,23 @@
 
 
 def tile_kernel(
-    n_core, n_col, side, count_s, rows_h, cols_h, ener_h, tiles, *refs,
+    n_core, n_col, side, count_s, rows_h, cols_h, ener_h, vec_h, tiles, *refs,
 ):
     gath, refs = refs[:n_core], refs[n_core:]
-    (own_ref, send_ref, rest_ref, rows_s, cols_s, ener,
+    (own_ref, send_ref, rest_ref, rows_s, cols_s, ener, vec,
      buf, table, picked, select, part, sems, small, *acc) = refs
-    n_far, kvec, own = gath[0].shape
+    kvec, own = vec.shape
+    n_row = gath[0].shape[0]
     slots = tiles.shape[0]
     blk_own = own // side
     per = LANES // side
     n_chunk = tiles.shape[1] // LANES
-    my_far, my_core, my_col = (lax.axis_index(name) for name in ("far", "core", "col"))
+    my_core, my_col = lax.axis_index("core"), lax.axis_index("col")
 
     copies = [
         pltpu.make_async_copy(src, dst, small.at[i])
         for i, (src, dst) in enumerate(
-            ((cols_h, cols_s), (rows_h, rows_s), (ener_h, ener))
+            ((cols_h, cols_s), (rows_h, rows_s), (ener_h, ener), (vec_h, vec))
         )
     ]
     for copy in copies:
@@ -56,18 +57,19 @@
     low = lane < side
     zero = jnp.zeros((kvec, LANES), jnp.float32)
 
+    half = own // n_core
     for s in range(n_core):
-        core = lax.rem(my_core + (n_core - s), n_core)
-        for f in range(n_far):
-            for p in range(own // LANES):
-                x = gath[s][f, :, p * LANES:(p + 1) * LANES].astype(jnp.float32)
+        part_of = lax.rem(my_core + (n_core - s), n_core) * (half // side)
+        for r in range(n_row):
+            for p in range(half // LANES):
+                x = gath[s][r, :, p * LANES:(p + 1) * LANES].astype(jnp.float32)
                 y = pltpu.roll(x, side, 1)
-                at = (f * n_core + core) * blk_own + p * per
+                at = r * blk_own + part_of + p * per
                 even = jnp.concatenate([jnp.where(low, x, zero), jnp.where(low, zero, y)], axis=0)
                 odd = jnp.concatenate([jnp.where(low, y, zero), jnp.where(low, zero, x)], axis=0)
                 table[at] = even
                 table[at + 1] = odd
-    n_blocks = n_far * n_core * blk_own
+    n_blocks = n_row * blk_own
     table[n_blocks] = jnp.zeros((per * kvec, LANES), jnp.float32)
 
     for copy in copies:
@@ -165,16 +167,17 @@
         c, lane0 = divmod(m * LANES, own)
         part[c, :, lane0:lane0 + LANES] = row
 
-    own_ref[...] = part[my_col] + ener[...] * gath[0][my_far].astype(jnp.float32)
+    own_ref[...] = part[my_col] + ener[...] * vec[...].astype(jnp.float32)
     for s in range(1, n_col):
         share = part[lax.rem(my_col + s, n_col)]
         send_ref[s - 1] = share.astype(jnp.bfloat16)
         rest_ref[s - 1] = share
 
 
-def tile_work(rows, cols, count, gath, n_col, ener, tiles):
+def tile_work(rows, cols, count, vec, gath, n_col, ener, tiles):
     n_core = len(gath)
-    n_far, kvec, own = gath[0].shape
+    kvec, own = vec.shape
+    n_row = gath[0].shape[0]
     slots, area = tiles.shape
     side = math.isqrt(area)
     per = LANES // side
@@ -190,26 +193,27 @@
             jax.ShapeDtypeStruct((n_col - 1, kvec, own), jnp.bfloat16),
             jax.ShapeDtypeStruct((n_col - 1, kvec, own), jnp.float32),
         ),
-        in_specs=[pl.BlockSpec(memory_space=pltpu.SMEM)] + [far_away] * 4 + [vmem] * n_core,
+        in_specs=[pl.BlockSpec(memory_space=pltpu.SMEM)] + [far_away] * 5 + [vmem] * n_core,
         out_specs=(vmem, vmem, vmem),
         scratch_shapes=[
             pltpu.SMEM((slots,), jnp.int32),
             pltpu.SMEM((slots,), jnp.int32),
             pltpu.VMEM((1, own), jnp.float32),
+            pltpu.VMEM((kvec, own), jnp.bfloat16),
             pltpu.VMEM((slots, area), jnp.bfloat16),
-            pltpu.VMEM((n_far * n_core * blk_own + 1, per * kvec, LANES), jnp.float32),
+            pltpu.VMEM((n_row * blk_own + 1, per * kvec, LANES), jnp.float32),
             pltpu.VMEM((n_seg // per * 2 * kvec, per * per * width), jnp.bfloat16),
             pltpu.VMEM((per * per * width, LANES), jnp.bfloat16),
             pltpu.VMEM((n_col, kvec, own), jnp.float32),
             pltpu.SemaphoreType.DMA((slots // CHUNK,)),
-            pltpu.SemaphoreType.DMA((3,)),
+            pltpu.SemaphoreType.DMA((4,)),
         ] + [pltpu.VMEM((n_seg, per * kvec, width), jnp.float32)] * SUMS,
         compiler_params=pltpu.CompilerParams(vmem_limit_bytes=48 * 2**20),
         cost_estimate=pl.CostEstimate(
             flops=2 * slots * area * kvec, bytes_accessed=2 * slots * area, transcendentals=0
         ),
         name="tile_work",
-    )(count, *[pltpu.with_memory_space_constraint(x, pltpu.HBM) for x in (rows, cols, ener, tiles)],
+    )(count, *[pltpu.with_memory_space_constraint(x, pltpu.HBM) for x in (rows, cols, ener, vec, tiles)],
       *gath)
 
 
@@ -292,11 +296,14 @@
 def per_device(vectors, energies, tiles, tile_rows, tile_cols, tile_count):
     kvec, own = vectors.shape
     n_col = lax.axis_size("col")
-    copies = jnp.broadcast_to(vectors[None], (lax.axis_size("far"), kvec, own))
-    gath = lax.all_to_all(copies, "far", 0, 0)
+    n_core = lax.axis_size("core")
+    n_row = lax.axis_size("far") * n_core
+    halves = vectors.reshape(kvec, n_core, own // n_core).swapaxes(0, 1)
+    copies = jnp.broadcast_to(halves[None], (n_row // n_core,) + halves.shape)
+    gath = lax.all_to_all(copies.reshape((n_row,) + halves.shape[1:]), ("far", "core"), 0, 0)
     gath = from_all(gath, "core")
     base, send, rest = tile_work(
-        tile_rows, tile_cols, tile_count, gath, n_col, energies[None, :], tiles
+        tile_rows, tile_cols, tile_count, vectors, gath, n_col, energies[None, :], tiles
     )
     got = [
         lax.ppermute(send[s - 1], "col", [(c, (c + s) % n_col) for c in range(n_col)])

time: 34 us -> 34.6 us (1.018)
  starting transfers between devices: 5.78 us -> 6.95 us
  Pallas kernels: 5.2 us -> 4.05 us
  blocking collectives: 14.4 us -> 15.1 us
    pallas_call x1, Pallas kernels: 4.13 us -> 2.99 us  [tile_work(): pl.pallas_call(functools.partial(tile_kernel, n_core, n_col, side), out_s...]
    all_to_all x1, starting transfers between devices: 2.54 us -> 3.6 us  [per_device(): gram_parts = lax.all_to_all(terms, ('far', 'core', 'col'), 0, 0)]
    all_to_all x1, blocking collectives: 14.4 us -> 15.1 us  [per_device(): lax.all_to_all(copies.reshape((n_row,) + halves.shape[1:]), ('far', 'core...]
  transfers between devices with their start and end apart: 4 -> 4, of which waited for: 2 -> 2; matrix products, arithmetic and copies ran while one was open for 0% -> 0% of each run, Pallas kernels for 12% -> 9%
where the time goes in v3:
time: 34.6 us; the launch traced here: 34.2 us
  blocking collectives  15.1 us (44%)
  starting transfers between devices  6.95 us (20%)
  waiting for transfers between devices  5.29 us (15%)
  Pallas kernels  4.05 us (12%)
  local copies, waits for them, and re-layouts  1.43 us (4%)
  between operations  1.33 us (4%)
    all_to_all x1, blocking collectives, per_device(): lax.all_to_all(copies.reshape((n_row,) + halves.shape[1:]), ('far', 'core...  15.1 us
    all_to_all x1, starting transfers between devices, per_device(): gram_parts = lax.all_to_all(terms, ('far', 'core', 'col'), 0, 0)  3.6 us
    all_to_all x1, waiting for transfers between devices, per_device(): gram_parts = lax.all_to_all(terms, ('far', 'core', 'col'), 0, 0)  3.3 us
    pallas_call x1, Pallas kernels, tile_work(): pl.pallas_call(functools.partial(tile_kernel, n_core, n_col, side), out_s...  2.99 us
    ppermute x1, waiting for transfers between devices, per_device(): lax.ppermute(send[s - 1], 'col', [(c, (c + s) % n_col) for c in range(n_c...  1.99 us
    ppermute x1, starting transfers between devices, per_device(): lax.ppermute(send[s - 1], 'col', [(c, (c + s) % n_col) for c in range(n_c...  1.83 us
    ppermute x2, starting transfers between devices, from_all(): lax.ppermute(x, axis, [(i, (i + s) % size) for i in range(size)])  1.52 us
    broadcast_in_dim x1, local copies, waits for them, and re-layouts, per_device(): copies = jnp.broadcast_to(halves[None], (n_row // n_core,) + halves.shape)  0.79 us
  transfers between devices with their start and end apart: 4, of which 2 were waited for; matrix products, arithmetic and copies ran while one was open for 0% of the time, Pallas kernels for 9%

profile of v3, /device:TPU:0, one launch (start us, length us, event | category | flops | bytes accessed | tf_op | source)
XLA Modules:
  0.0 34.2 jit_solution(1161440011996112337)
XLA Ops:
  0.6 0.0 copy-start
  0.6 0.8 %broadcast_in_dim.18 = bf16[8,2,8,512]{3,2,1,0:T(8,128)(2,1)S(1)} broadcast(bf16[2,8,512]{2,1,0:T(8,128)(2,1)} %bitcast.7), dimensions={1,2,3} | broadcast | bytes 147456 | tf_op jit(solution)/shard_map/broadcast_in_dim | solution.py:302
  1.4 15.1 %all_to_all.10.refs_0_ = bf16[16,8,512]{2,1,0:T(8,128)(2,1)S(1)} all-to-all(bf16[16,8,512]{2,1,0:T(8,128)(2,1)S(1)} %bitcast.10), channel_id=1, replica_groups=mesh['far'=8,'core'=2,'col'=2] {'far','core'}, dimensions={0} | all-to-all | bytes 262144 | tf_op jit(solution)/shard_map/all_to_all | solution.py:303
  16.5 0.0 collective-permute-start
  16.5 1.5 %collective-permute-start.1 = (bf16[8,1024]{1,0:T(8,128)(2,1)}, bf16[8,1024]{1,0:T(8,128)(2,1)S(1)}, u32[]{:S(2)}, u32[]{:S(2)}) collective-permute-start(bf16[8,1024]{1,0:T(8,128)(2,1)} %vec.3), channel_id=1, source_target_pairs={{0,1},{1,0},{2,3},{3,2},{4,5},{5,4},{6,7},{7,6},{8,9},{9,8},{10,11... | collective-permute-start | bytes 49160 | tf_op jit(solution)/shard_map/ppermute | solution.py:292
  18.7 0.0 collective-permute-done.refs_1_
  18.7 3.0 %tile_work.1 = (f32[8,1024]{1,0:T(8,128)S(1)}, bf16[1,8,1024]{2,1,0:T(8,128)(2,1)S(1)}, f32[1,8,1024]{2,1,0:T(8,128)S(1)}) custom-call(s32[1]{0:T(128)S(6)} %copy.8.count_s, s32[1024]{0:T(1024)} %rows_h.1, s32[1024]{0:T(1024)} %cols_h.1, f32[1,1024]{1,0:T(1,128)} %bitcast.11, bf16[8,1024]{1,0:T(8,128)(2,1)} %vec.3, bf16[1024,4096]{1,0:T(8,128)(2,1)} %tiles.1, ...), custom_call_target="tpu_custom_call" | custom-call | flops 67108864 | bytes 8388608 | tf_op jit(solution)/shard_map/tile_work/pallas_call | solution.py:189
  21.7 0.0 collective-permute-done.1.refs_0_
  21.7 0.0 copy-done
  21.7 0.3 gram_terms.1
  22.0 0.6 %broadcast_in_dim.20 = f32[32,1,128]{2,1,0:T(1,128)} broadcast(f32[128]{0:T(128)S(1)} %bitcast.8), dimensions={2} | broadcast | bytes 16896 | tf_op jit(solution)/shard_map/broadcast_in_dim | solution.py:315
  22.7 3.6 %all-to-all-start.1 = ((f32[32,1,128]{2,1,0:T(1,128)}), f32[32,1,128]{2,1,0:T(1,128)S(1)}, u32[]{:S(2)}, u32[]{:S(2)}) async-start(f32[32,1,128]{2,1,0:T(1,128)} %broadcast_in_dim.20), calls=%async_computation.1 | async-start | bytes 32768 | tf_op jit(solution)/shard_map/all_to_all | solution.py:316
  26.3 1.8 %collective-permute-start.2 = (bf16[8,1024]{1,0:T(8,128)(2,1)S(1)}, bf16[8,1024]{1,0:T(8,128)(2,1)S(1)}, u32[]{:S(2)}, u32[]{:S(2)}) collective-permute-start(bf16[8,1024]{1,0:T(8,128)(2,1)S(1)} %bitcast.9), channel_id=1, source_target_pairs={{0,1},{1,0},{2,3},{3,2},{4,5},{5,4},{6,7},{7,6},{8,9},{9,8},{10,11... | collective-permute-start | bytes 49160 | tf_op jit(solution)/shard_map/ppermute | solution.py:309
  28.1 2.0 %collective-permute-done.2.refs_0_ = bf16[8,1024]{1,0:T(8,128)(2,1)S(1)} collective-permute-done((bf16[8,1024]{1,0:T(8,128)(2,1)S(1)}, bf16[8,1024]{1,0:T(8,128)(2,1)S(1)}, u32[]{:S(2)}, u32[]{:S(2)}) %collective-permute-start.2) | collective-permute-done | bytes 16416 | tf_op jit(solution)/shard_map/ppermute | solution.py:309
  30.1 3.3 %all-to-all-done.1.gram_parts = f32[32,1,128]{2,1,0:T(1,128)S(1)} async-done(((f32[32,1,128]{2,1,0:T(1,128)}), f32[32,1,128]{2,1,0:T(1,128)S(1)}, u32[]{:S(2)}, u32[]{:S(2)}) %all-to-all-start.1) | async-done | bytes 16416 | tf_op jit(solution)/shard_map/all_to_all | solution.py:316
  33.4 0.8 %finish.1 = (bf16[8,1024]{1,0:T(8,128)(2,1)}, f32[8,1024]{1,0:T(8,128)}) custom-call(f32[8,1024]{1,0:T(8,128)S(1)} %get-tuple-element.5.own.base, f32[32,1,128]{2,1,0:T(1,128)S(1)} %all-to-all-done.1.gram_parts, bf16[8,1024]{1,0:T(8,128)(2,1)S(1)} %copy-done, bf16[8,1024]{1,0:T(8,128)(2,1)S(1)} %collective-permute-done.2.refs_0_), custom_call_target="tpu_custom_call" | custom-call | tf_op jit(solution)/shard_map/finish/pallas_call | solution.py:275
Async XLA Ops:
  0.6 21.1 %copy-start = (bf16[8,1024]{1,0:T(8,128)(2,1)S(1)}, bf16[8,1024]{1,0:T(8,128)(2,1)}, u32[]{:S(2)}) copy-start(bf16[8,1024]{1,0:T(8,128)(2,1)} %vec.3) | copy-start | bytes 49156
  16.5 2.2 %collective-permute-start = (bf16[16,8,512]{2,1,0:T(8,128)(2,1)S(1)}, bf16[16,8,512]{2,1,0:T(8,128)(2,1)S(1)}, u32[]{:S(2)}, u32[]{:S(2)}) collective-permute-start(bf16[16,8,512]{2,1,0:T(8,128)(2,1)S(1)} %all_to_all.10.refs_0_), channel_id=1, source_target_pairs={{0,2},{2,0},{1,3},{3,1},{4,6},{6,4},{5,7},{7,5},{8,10},{10,8},{9,1... | collective-permute-start | bytes 393224 | tf_op jit(solution)/shard_map/ppermute | solution.py:292
  16.5 5.2 %collective-permute-start.1 = (bf16[8,1024]{1,0:T(8,128)(2,1)}, bf16[8,1024]{1,0:T(8,128)(2,1)S(1)}, u32[]{:S(2)}, u32[]{:S(2)}) collective-permute-start(bf16[8,1024]{1,0:T(8,128)(2,1)} %vec.3), channel_id=1, source_target_pairs={{0,1},{1,0},{2,3},{3,2},{4,5},{5,4},{6,7},{7,6},{8,9},{9,8},{10,11... | collective-permute-start | bytes 49160 | tf_op jit(solution)/shard_map/ppermute | solution.py:292
  22.7 10.7 %all-to-all-start.1 = ((f32[32,1,128]{2,1,0:T(1,128)}), f32[32,1,128]{2,1,0:T(1,128)S(1)}, u32[]{:S(2)}, u32[]{:S(2)}) async-start(f32[32,1,128]{2,1,0:T(1,128)} %broadcast_in_dim.20), calls=%async_computation.1 | async-start | bytes 32768 | tf_op jit(solution)/shard_map/all_to_all | solution.py:316
  26.3 3.8 %collective-permute-start.2 = (bf16[8,1024]{1,0:T(8,128)(2,1)S(1)}, bf16[8,1024]{1,0:T(8,128)(2,1)S(1)}, u32[]{:S(2)}, u32[]{:S(2)}) collective-permute-start(bf16[8,1024]{1,0:T(8,128)(2,1)S(1)} %bitcast.9), channel_id=1, source_target_pairs={{0,1},{1,0},{2,3},{3,2},{4,5},{5,4},{6,7},{7,6},{8,9},{9,8},{10,11... | collective-permute-start | bytes 49160 | tf_op jit(solution)/shard_map/ppermute | solution.py:309

commit v4 on v3

--- a/solution.py
+++ b/solution.py
@@ -6,7 +6,7 @@
 from jax import lax
 from jax.experimental import pallas as pl
 from jax.experimental.pallas import tpu as pltpu
-from jax.sharding import Mesh, PartitionSpec as P
+from jax.sharding import PartitionSpec as P
 
 LANES = 128
 SUB = 8
@@ -29,7 +29,7 @@
     blk_own = own // side
     per = LANES // side
     n_chunk = tiles.shape[1] // LANES
-    my_core, my_col = lax.axis_index("core"), lax.axis_index("col")
+    my_core, my_col = lax.axis_index("row") % n_core, lax.axis_index("col")
 
     copies = [
         pltpu.make_async_copy(src, dst, small.at[i])
@@ -285,23 +285,23 @@
     )(base, gram_parts, vectors, *got)
 
 
-def from_all(x, axis):
-    size = lax.axis_size(axis)
+def from_all(x, axis, group):
     got = [x]
-    for s in range(1, size):
-        got.append(lax.ppermute(x, axis, [(i, (i + s) % size) for i in range(size)]))
+    for s in range(1, group):
+        perm = [(i, i - i % group + (i + s) % group) for i in range(lax.axis_size(axis))]
+        got.append(lax.ppermute(x, axis, perm))
     return got
 
 
 def per_device(vectors, energies, tiles, tile_rows, tile_cols, tile_count):
     kvec, own = vectors.shape
     n_col = lax.axis_size("col")
-    n_core = lax.axis_size("core")
-    n_row = lax.axis_size("far") * n_core
+    n_row = lax.axis_size("row")
+    n_core = 2 if n_row % 2 == 0 else 1
     halves = vectors.reshape(kvec, n_core, own // n_core).swapaxes(0, 1)
     copies = jnp.broadcast_to(halves[None], (n_row // n_core,) + halves.shape)
-    gath = lax.all_to_all(copies.reshape((n_row,) + halves.shape[1:]), ("far", "core"), 0, 0)
-    gath = from_all(gath, "core")
+    gath = lax.all_to_all(copies.reshape((n_row,) + halves.shape[1:]), "row", 0, 0)
+    gath = from_all(gath, "row", n_core)
     base, send, rest = tile_work(
         tile_rows, tile_cols, tile_count, vectors, gath, n_col, energies[None, :], tiles
     )
@@ -309,21 +309,24 @@
         lax.ppermute(send[s - 1], "col", [(c, (c + s) % n_col) for c in range(n_col)])
         for s in range(1, n_col)
     ]
-    others = from_all(vectors, "col")[1:]
-    members = lax.axis_size(("far", "core", "col"))
+    others = from_all(vectors, "col", n_col)[1:]
+    members = n_row * n_col
     terms = gram_terms(base, rest, vectors, others)
     terms = jnp.broadcast_to(terms[None], (members,) + terms.shape)
-    gram_parts = lax.all_to_all(terms, ("far", "core", "col"), 0, 0)
+    gram_parts = lax.all_to_all(terms, ("row", "col"), 0, 0)
     return finish(1.0 / (members * own), base, gram_parts, vectors, got)
 
 
 def solution(mesh):
-    n_row, n_col = mesh.devices.shape
-    n_core = 2 if n_row % 2 == 0 else 1
-    split = ("far", "core", "col")
-    chips = Mesh(mesh.devices.reshape(n_row // n_core, n_core, n_col), split)
-    in_specs = (P(None, split), P(split), P(split, None), P(split), P(split), P(split))
-    out_specs = (P(None, split), P(None, split))
+    in_specs = (
+        P(None, ("row", "col")),
+        P(("row", "col")),
+        P(("row", "col"), None),
+        P(("row", "col")),
+        P(("row", "col")),
+        P(("row", "col")),
+    )
+    out_specs = (P(None, ("row", "col")), P(None, ("row", "col")))
     return jax.shard_map(
-        per_device, mesh=chips, in_specs=in_specs, out_specs=out_specs, check_vma=False
+        per_device, mesh=mesh, in_specs=in_specs, out_specs=out_specs, check_vma=False
     )

time: 34.6 us -> 34.8 us (level)
  starting transfers between devices: 6.95 us -> 7.41 us
    all_to_all x1, starting transfers between devices: 3.6 us -> 4.06 us  [per_device(): gram_parts = lax.all_to_all(terms, ('row', 'col'), 0, 0)]
where the time goes in v4:
time: 34.8 us; the launch traced here: 34.6 us
  blocking collectives  15.1 us (43%)
  starting transfers between devices  7.41 us (21%)
  waiting for transfers between devices  5.29 us (15%)
  Pallas kernels  4.05 us (12%)
  local copies, waits for them, and re-layouts  1.43 us (4%)
  between operations  1.33 us (4%)
    all_to_all x1, blocking collectives, per_device(): lax.all_to_all(copies.reshape((n_row,) + halves.shape[1:]), 'row', 0, 0)  15.1 us
    all_to_all x1, starting transfers between devices, per_device(): gram_parts = lax.all_to_all(terms, ('row', 'col'), 0, 0)  4.06 us
    all_to_all x1, waiting for transfers between devices, per_device(): gram_parts = lax.all_to_all(terms, ('row', 'col'), 0, 0)  3.3 us
    pallas_call x1, Pallas kernels, tile_work(): pl.pallas_call(functools.partial(tile_kernel, n_core, n_col, side), out_s...  2.99 us
    ppermute x1, waiting for transfers between devices, per_device(): lax.ppermute(send[s - 1], 'col', [(c, (c + s) % n_col) for c in range(n_c...  1.99 us
    ppermute x1, starting transfers between devices, per_device(): lax.ppermute(send[s - 1], 'col', [(c, (c + s) % n_col) for c in range(n_c...  1.83 us
    ppermute x2, starting transfers between devices, from_all(): got.append(lax.ppermute(x, axis, perm))  1.52 us
    broadcast_in_dim x1, local copies, waits for them, and re-layouts, per_device(): copies = jnp.broadcast_to(halves[None], (n_row // n_core,) + halves.shape)  0.79 us
  transfers between devices with their start and end apart: 4, of which 2 were waited for; matrix products, arithmetic and copies ran while one was open for 0% of the time, Pallas kernels for 9%

profile of v4, /device:TPU:0, one launch (start us, length us, event | category | flops | bytes accessed | tf_op | source)
XLA Modules:
  0.0 34.6 jit_solution(2391625564183126915)
XLA Ops:
  0.6 0.0 copy-start
  0.6 0.8 %broadcast_in_dim.18 = bf16[8,2,8,512]{3,2,1,0:T(8,128)(2,1)S(1)} broadcast(bf16[2,8,512]{2,1,0:T(8,128)(2,1)} %bitcast.7), dimensions={1,2,3} | broadcast | bytes 147456 | tf_op jit(solution)/shard_map/broadcast_in_dim | solution.py:302
  1.4 15.1 %all_to_all.10.refs_0_ = bf16[16,8,512]{2,1,0:T(8,128)(2,1)S(1)} all-to-all(bf16[16,8,512]{2,1,0:T(8,128)(2,1)S(1)} %bitcast.10), channel_id=1, replica_groups=mesh['row'=16,'col'=2] {'row'}, dimensions={0} | all-to-all | bytes 262144 | tf_op jit(solution)/shard_map/all_to_all | solution.py:303
  16.5 0.0 collective-permute-start
  16.5 1.5 %collective-permute-start.1 = (bf16[8,1024]{1,0:T(8,128)(2,1)}, bf16[8,1024]{1,0:T(8,128)(2,1)S(1)}, u32[]{:S(2)}, u32[]{:S(2)}) collective-permute-start(bf16[8,1024]{1,0:T(8,128)(2,1)} %vec.3), channel_id=1, source_target_pairs={{0,1},{1,0},{2,3},{3,2},{4,5},{5,4},{6,7},{7,6},{8,9},{9,8},{10,11... | collective-permute-start | bytes 49160 | tf_op jit(solution)/shard_map/ppermute | solution.py:292
  18.7 0.0 collective-permute-done.refs_1_
  18.7 3.0 %tile_work.1 = (f32[8,1024]{1,0:T(8,128)S(1)}, bf16[1,8,1024]{2,1,0:T(8,128)(2,1)S(1)}, f32[1,8,1024]{2,1,0:T(8,128)S(1)}) custom-call(s32[1]{0:T(128)S(6)} %copy.8.count_s, s32[1024]{0:T(1024)} %rows_h.1, s32[1024]{0:T(1024)} %cols_h.1, f32[1,1024]{1,0:T(1,128)} %bitcast.11, bf16[8,1024]{1,0:T(8,128)(2,1)} %vec.3, bf16[1024,4096]{1,0:T(8,128)(2,1)} %tiles.1, ...), custom_call_target="tpu_custom_call" | custom-call | flops 67108864 | bytes 8388608 | tf_op jit(solution)/shard_map/tile_work/pallas_call | solution.py:189
  21.7 0.0 collective-permute-done.1.refs_0_
  21.7 0.0 copy-done
  21.7 0.3 gram_terms.1
  22.0 0.6 %broadcast_in_dim.20 = f32[32,1,128]{2,1,0:T(1,128)} broadcast(f32[128]{0:T(128)S(1)} %bitcast.8), dimensions={2} | broadcast | bytes 16896 | tf_op jit(solution)/shard_map/broadcast_in_dim | solution.py:315
  22.7 4.1 %all-to-all-start.1 = ((f32[32,1,128]{2,1,0:T(1,128)}), f32[32,1,128]{2,1,0:T(1,128)S(1)}, u32[]{:S(2)}, u32[]{:S(2)}) async-start(f32[32,1,128]{2,1,0:T(1,128)} %broadcast_in_dim.20), calls=%async_computation.1 | async-start | bytes 32768 | tf_op jit(solution)/shard_map/all_to_all | solution.py:316
  26.7 1.8 %collective-permute-start.2 = (bf16[8,1024]{1,0:T(8,128)(2,1)S(1)}, bf16[8,1024]{1,0:T(8,128)(2,1)S(1)}, u32[]{:S(2)}, u32[]{:S(2)}) collective-permute-start(bf16[8,1024]{1,0:T(8,128)(2,1)S(1)} %bitcast.9), channel_id=1, source_target_pairs={{0,1},{1,0},{2,3},{3,2},{4,5},{5,4},{6,7},{7,6},{8,9},{9,8},{10,11... | collective-permute-start | bytes 49160 | tf_op jit(solution)/shard_map/ppermute | solution.py:309
  28.6 2.0 %collective-permute-done.2.refs_0_ = bf16[8,1024]{1,0:T(8,128)(2,1)S(1)} collective-permute-done((bf16[8,1024]{1,0:T(8,128)(2,1)S(1)}, bf16[8,1024]{1,0:T(8,128)(2,1)S(1)}, u32[]{:S(2)}, u32[]{:S(2)}) %collective-permute-start.2) | collective-permute-done | bytes 16416 | tf_op jit(solution)/shard_map/ppermute | solution.py:309
  30.6 3.3 %all-to-all-done.1.gram_parts = f32[32,1,128]{2,1,0:T(1,128)S(1)} async-done(((f32[32,1,128]{2,1,0:T(1,128)}), f32[32,1,128]{2,1,0:T(1,128)S(1)}, u32[]{:S(2)}, u32[]{:S(2)}) %all-to-all-start.1) | async-done | bytes 16416 | tf_op jit(solution)/shard_map/all_to_all | solution.py:316
  33.9 0.8 %finish.1 = (bf16[8,1024]{1,0:T(8,128)(2,1)}, f32[8,1024]{1,0:T(8,128)}) custom-call(f32[8,1024]{1,0:T(8,128)S(1)} %get-tuple-element.5.own.base, f32[32,1,128]{2,1,0:T(1,128)S(1)} %all-to-all-done.1.gram_parts, bf16[8,1024]{1,0:T(8,128)(2,1)S(1)} %copy-done, bf16[8,1024]{1,0:T(8,128)(2,1)S(1)} %collective-permute-done.2.refs_0_), custom_call_target="tpu_custom_call" | custom-call | tf_op jit(solution)/shard_map/finish/pallas_call | solution.py:275
Async XLA Ops:
  0.6 21.1 %copy-start = (bf16[8,1024]{1,0:T(8,128)(2,1)S(1)}, bf16[8,1024]{1,0:T(8,128)(2,1)}, u32[]{:S(2)}) copy-start(bf16[8,1024]{1,0:T(8,128)(2,1)} %vec.3) | copy-start | bytes 49156
  16.5 2.2 %collective-permute-start = (bf16[16,8,512]{2,1,0:T(8,128)(2,1)S(1)}, bf16[16,8,512]{2,1,0:T(8,128)(2,1)S(1)}, u32[]{:S(2)}, u32[]{:S(2)}) collective-permute-start(bf16[16,8,512]{2,1,0:T(8,128)(2,1)S(1)} %all_to_all.10.refs_0_), channel_id=1, source_target_pairs={{0,2},{2,0},{4,6},{6,4},{8,10},{10,8},{12,14},{14,12},{16,18},{18,... | collective-permute-start | bytes 393224 | tf_op jit(solution)/shard_map/ppermute | solution.py:292
  16.5 5.2 %collective-permute-start.1 = (bf16[8,1024]{1,0:T(8,128)(2,1)}, bf16[8,1024]{1,0:T(8,128)(2,1)S(1)}, u32[]{:S(2)}, u32[]{:S(2)}) collective-permute-start(bf16[8,1024]{1,0:T(8,128)(2,1)} %vec.3), channel_id=1, source_target_pairs={{0,1},{1,0},{2,3},{3,2},{4,5},{5,4},{6,7},{7,6},{8,9},{9,8},{10,11... | collective-permute-start | bytes 49160 | tf_op jit(solution)/shard_map/ppermute | solution.py:292
  22.7 11.2 %all-to-all-start.1 = ((f32[32,1,128]{2,1,0:T(1,128)}), f32[32,1,128]{2,1,0:T(1,128)S(1)}, u32[]{:S(2)}, u32[]{:S(2)}) async-start(f32[32,1,128]{2,1,0:T(1,128)} %broadcast_in_dim.20), calls=%async_computation.1 | async-start | bytes 32768 | tf_op jit(solution)/shard_map/all_to_all | solution.py:316
  26.7 3.8 %collective-permute-start.2 = (bf16[8,1024]{1,0:T(8,128)(2,1)S(1)}, bf16[8,1024]{1,0:T(8,128)(2,1)S(1)}, u32[]{:S(2)}, u32[]{:S(2)}) collective-permute-start(bf16[8,1024]{1,0:T(8,128)(2,1)S(1)} %bitcast.9), channel_id=1, source_target_pairs={{0,1},{1,0},{2,3},{3,2},{4,5},{5,4},{6,7},{7,6},{8,9},{9,8},{10,11... | collective-permute-start | bytes 49160 | tf_op jit(solution)/shard_map/ppermute | solution.py:309

commit v5 on v2

--- a/solution.py
+++ b/solution.py
@@ -17,12 +17,19 @@
 NT = (((1,), (1,)), ((), ()))
 
 
+def outer(share, seg):
+    return lax.dot_general(
+        share, seg, NT, precision=lax.Precision.HIGHEST, preferred_element_type=jnp.float32
+    )
+
+
 def tile_kernel(
     n_core, n_col, side, count_s, rows_h, cols_h, ener_h, tiles, *refs,
 ):
     gath, refs = refs[:n_core], refs[n_core:]
-    (own_ref, send_ref, rest_ref, rows_s, cols_s, ener,
-     buf, table, picked, select, part, sems, small, *acc) = refs
+    others, refs = refs[:n_col - 1], refs[n_col - 1:]
+    (own_ref, send_ref, terms_ref, rows_s, cols_s, ener,
+     buf, table, picked, select, part, wide, sems, small, *acc) = refs
     n_far, kvec, own = gath[0].shape
     slots = tiles.shape[0]
     blk_own = own // side
@@ -80,7 +87,7 @@
             a[r] = jnp.zeros(a.shape[1:], jnp.float32)
         return carry
 
-    lax.fori_loop(0, n_seg, clear, 0)
+    lax.fori_loop(0, n_seg, clear, 0, unroll=4)
 
     k_id = lax.broadcasted_iota(jnp.int32, (width, LANES), 0)
     n_id = lax.broadcasted_iota(jnp.int32, (width, LANES), 1)
@@ -156,7 +163,7 @@
         picked[pl.ds(pl.multiple_of(m * 2 * kvec, 2 * kvec), 2 * kvec), :] = both
         return carry
 
-    lax.fori_loop(0, pairs, pick, 0)
+    lax.fori_loop(0, pairs, pick, 0, unroll=4)
 
     spread = jnp.dot(picked[...], select[...], preferred_element_type=jnp.float32)
     for m in range(pairs):
@@ -165,15 +172,24 @@
         c, lane0 = divmod(m * LANES, own)
         part[c, :, lane0:lane0 + LANES] = row
 
-    own_ref[...] = part[my_col] + ener[...] * gath[0][my_far].astype(jnp.float32)
+    vec = gath[0][my_far].astype(jnp.float32)
+    mine = part[my_col] + ener[...] * vec
+    own_ref[...] = mine
+    terms = outer(mine, vec)
     for s in range(1, n_col):
         share = part[lax.rem(my_col + s, n_col)]
         send_ref[s - 1] = share.astype(jnp.bfloat16)
-        rest_ref[s - 1] = share
-
-
-def tile_work(rows, cols, count, gath, n_col, ener, tiles):
-    n_core = len(gath)
+        terms = terms + outer(share, others[n_col - s - 1][...].astype(jnp.float32))
+    wide[...] = jnp.zeros(wide.shape, jnp.float32)
+    wide[:, :kvec] = terms
+    spaced = pltpu.roll(wide[...], 0, 1, stride=kvec, stride_axis=0)
+    flat = jnp.sum(spaced, axis=0, keepdims=True)
+    for i in range(terms_ref.shape[0]):
+        terms_ref[i] = flat
+
+
+def tile_work(rows, cols, count, gath, others, members, ener, tiles):
+    n_core, n_col = len(gath), len(others) + 1
     n_far, kvec, own = gath[0].shape
     slots, area = tiles.shape
     side = math.isqrt(area)
@@ -188,9 +204,9 @@
         out_shape=(
             jax.ShapeDtypeStruct((kvec, own), jnp.float32),
             jax.ShapeDtypeStruct((n_col - 1, kvec, own), jnp.bfloat16),
-            jax.ShapeDtypeStruct((n_col - 1, kvec, own), jnp.float32),
+            jax.ShapeDtypeStruct((members, 1, LANES), jnp.float32),
         ),
-        in_specs=[pl.BlockSpec(memory_space=pltpu.SMEM)] + [far_away] * 4 + [vmem] * n_core,
+        in_specs=[pl.BlockSpec(memory_space=pltpu.SMEM)] + [far_away] * 4 + [vmem] * (n_core + n_col - 1),
         out_specs=(vmem, vmem, vmem),
         scratch_shapes=[
             pltpu.SMEM((slots,), jnp.int32),
@@ -201,6 +217,7 @@
             pltpu.VMEM((n_seg // per * 2 * kvec, per * per * width), jnp.bfloat16),
             pltpu.VMEM((per * per * width, LANES), jnp.bfloat16),
             pltpu.VMEM((n_col, kvec, own), jnp.float32),
+            pltpu.VMEM((kvec, LANES), jnp.float32),
             pltpu.SemaphoreType.DMA((slots // CHUNK,)),
             pltpu.SemaphoreType.DMA((3,)),
         ] + [pltpu.VMEM((n_seg, per * kvec, width), jnp.float32)] * SUMS,
@@ -210,40 +227,7 @@
         ),
         name="tile_work",
     )(count, *[pltpu.with_memory_space_constraint(x, pltpu.HBM) for x in (rows, cols, ener, tiles)],
-      *gath)
-
-
-def terms_kernel(own, rest, vec, *refs):
-    others, (terms_ref, wide) = refs[:-2], refs[-2:]
-    n_col = len(others) + 1
-    kvec = vec.shape[0]
-
-    def outer(share, seg):
-        return lax.dot_general(
-            share, seg[...].astype(jnp.float32), NT,
-            precision=lax.Precision.HIGHEST, preferred_element_type=jnp.float32,
-        )
-
-    terms = outer(own[...], vec)
-    for s in range(1, n_col):
-        terms = terms + outer(rest[s - 1], others[n_col - s - 1])
-    wide[...] = jnp.zeros(wide.shape, jnp.float32)
-    wide[:, :kvec] = terms
-    spaced = pltpu.roll(wide[...], 0, 1, stride=kvec, stride_axis=0)
-    terms_ref[...] = jnp.sum(spaced, axis=0, keepdims=True)
-
-
-def gram_terms(own, rest, vectors, others):
-    vmem = pl.BlockSpec(memory_space=pltpu.VMEM)
-    return pl.pallas_call(
-        terms_kernel,
-        out_shape=jax.ShapeDtypeStruct((1, LANES), jnp.float32),
-        in_specs=[vmem] * (3 + len(others)),
-        out_specs=vmem,
-        scratch_shapes=[pltpu.VMEM((vectors.shape[0], LANES), jnp.float32)],
-        compiler_params=pltpu.CompilerParams(vmem_limit_bytes=4 * 2**20),
-        name="gram_terms",
-    )(own, rest, vectors, *others)
+      *gath, *others)
 
 
 def finish_kernel(scale, base, gram_parts, vec, *refs):
@@ -294,18 +278,17 @@
     n_col = lax.axis_size("col")
     copies = jnp.broadcast_to(vectors[None], (lax.axis_size("far"), kvec, own))
     gath = lax.all_to_all(copies, "far", 0, 0)
+    others = from_all(vectors, "col")[1:]
+    gath, others = lax.optimization_barrier((gath, others))
     gath = from_all(gath, "core")
-    base, send, rest = tile_work(
-        tile_rows, tile_cols, tile_count, gath, n_col, energies[None, :], tiles
+    members = lax.axis_size(("far", "core", "col"))
+    base, send, terms = tile_work(
+        tile_rows, tile_cols, tile_count, gath, others, members, energies[None, :], tiles
     )
     got = [
         lax.ppermute(send[s - 1], "col", [(c, (c + s) % n_col) for c in range(n_col)])
         for s in range(1, n_col)
     ]
-    others = from_all(vectors, "col")[1:]
-    members = lax.axis_size(("far", "core", "col"))
-    terms = gram_terms(base, rest, vectors, others)
-    terms = jnp.broadcast_to(terms[None], (members,) + terms.shape)
     gram_parts = lax.all_to_all(terms, ("far", "core", "col"), 0, 0)
     return finish(1.0 / (members * own), base, gram_parts, vectors, got)
 

time: 34 us -> 35.5 us (1.044)
  blocking collectives: 14.4 us -> 0 us
  starting transfers between devices: 5.78 us -> 14.8 us
  waiting for transfers between devices: 5.41 us -> 11.8 us
  Pallas kernels: 5.2 us -> 5.81 us
    all_to_all x1 -> x0, blocking collectives: 14.4 us -> none  [per_device(): gath = lax.all_to_all(copies, 'far', 0, 0)]
    all_to_all x0 -> x1, starting transfers between devices: none -> 7.25 us  [per_device(): gath = lax.all_to_all(copies, 'far', 0, 0)]
    all_to_all x0 -> x1, waiting for transfers between devices: none -> 3.39 us  [per_device(): gath = lax.all_to_all(copies, 'far', 0, 0)]
    ppermute x2, waiting for transfers between devices: 0.01 us -> 3.12 us  [from_all(): lax.ppermute(x, axis, [(i, (i + s) % size) for i in range(size)])]
    all_to_all x1, starting transfers between devices: 2.54 us -> 4.16 us  [per_device(): gram_parts = lax.all_to_all(terms, ('far', 'core', 'col'), 0, 0)]
    pallas_call x1, Pallas kernels: 4.13 us -> 5.06 us  [tile_work(): pl.pallas_call(functools.partial(tile_kernel, n_core, n_col, side), out_s...]
    broadcast_in_dim x1, local copies, waits for them, and re-layouts: 0.79 us -> 1.44 us  [per_device(): copies = jnp.broadcast_to(vectors[None], (lax.axis_size('far'), kvec, own))]
    broadcast_in_dim x1 -> x0, local copies, waits for them, and re-layouts: 0.63 us -> none  [per_device(): terms = jnp.broadcast_to(terms[None], (members,) + terms.shape)]
  transfers between devices with their start and end apart: 4 -> 5, of which waited for: 2 -> 5; matrix products, arithmetic and copies ran while one was open for 0% -> 0% of each run, Pallas kernels for 12% -> 0%
where the time goes in v5:
time: 35.5 us; the launch traced here: 35.1 us
  starting transfers between devices  14.8 us (42%)
  waiting for transfers between devices  11.8 us (33%)
  Pallas kernels  5.81 us (16%)
  local copies, waits for them, and re-layouts  1.45 us (4%)
  between operations  1.31 us (4%)
    all_to_all x1, starting transfers between devices, per_device(): gath = lax.all_to_all(copies, 'far', 0, 0)  7.25 us
    pallas_call x1, Pallas kernels, tile_work(): pl.pallas_call(functools.partial(tile_kernel, n_core, n_col, side), out_s...  5.06 us
    all_to_all x1, starting transfers between devices, per_device(): gram_parts = lax.all_to_all(terms, ('far', 'core', 'col'), 0, 0)  4.16 us
    all_to_all x1, waiting for transfers between devices, per_device(): gath = lax.all_to_all(copies, 'far', 0, 0)  3.39 us
    all_to_all x1, waiting for transfers between devices, per_device(): gram_parts = lax.all_to_all(terms, ('far', 'core', 'col'), 0, 0)  3.3 us
    ppermute x2, waiting for transfers between devices, from_all(): lax.ppermute(x, axis, [(i, (i + s) % size) for i in range(size)])  3.12 us
    ppermute x1, waiting for transfers between devices, per_device(): lax.ppermute(send[s - 1], 'col', [(c, (c + s) % n_col) for c in range(n_c...  1.99 us
    ppermute x1, starting transfers between devices, per_device(): lax.ppermute(send[s - 1], 'col', [(c, (c + s) % n_col) for c in range(n_c...  1.83 us
  transfers between devices with their start and end apart: 5, of which 5 were waited for; matrix products, arithmetic and copies ran while one was open for 0% of the time, Pallas kernels for 0%

profile of v5, /device:TPU:0, one launch (start us, length us, event | category | flops | bytes accessed | tf_op | source)
XLA Modules:
  0.0 35.1 jit_solution(13748219491239552011)
XLA Ops:
  0.6 0.0 copy-start
  0.6 1.4 %broadcast_in_dim.10 = bf16[8,8,1024]{2,1,0:T(8,128)(2,1)} broadcast(bf16[8,1024]{1,0:T(8,128)(2,1)} %vec.1), dimensions={1,2} | broadcast | bytes 147456 | tf_op jit(solution)/shard_map/broadcast_in_dim | solution.py:279
  2.1 7.3 %all-to-all-start = ((bf16[8,8,1024]{2,1,0:T(8,128)(2,1)}), bf16[8,8,1024]{2,1,0:T(8,128)(2,1)S(1)}, u32[]{:S(2)}, u32[]{:S(2)}) async-start(bf16[8,8,1024]{2,1,0:T(8,128)(2,1)} %broadcast_in_dim.10), calls=%async_computation | async-start | bytes 262144 | tf_op jit(solution)/shard_map/all_to_all | solution.py:280
  9.3 1.5 %collective-permute-start = (bf16[8,1024]{1,0:T(8,128)(2,1)}, bf16[8,1024]{1,0:T(8,128)(2,1)S(1)}, u32[]{:S(2)}, u32[]{:S(2)}) collective-permute-start(bf16[8,1024]{1,0:T(8,128)(2,1)} %vec.1), channel_id=1, source_target_pairs={{0,1},{1,0},{2,3},{3,2},{4,5},{5,4},{6,7},{7,6},{8,9},{9,8},{10,11... | collective-permute-start | bytes 49160 | tf_op jit(solution)/shard_map/ppermute | solution.py:272
  10.9 2.4 %collective-permute-done.refs_2_ = bf16[8,1024]{1,0:T(8,128)(2,1)S(1)} collective-permute-done((bf16[8,1024]{1,0:T(8,128)(2,1)}, bf16[8,1024]{1,0:T(8,128)(2,1)S(1)}, u32[]{:S(2)}, u32[]{:S(2)}) %collective-permute-start) | collective-permute-done | bytes 16416 | tf_op jit(solution)/shard_map/ppermute | solution.py:272
  13.3 3.4 %all-to-all-done.refs_0_ = bf16[8,8,1024]{2,1,0:T(8,128)(2,1)S(1)} async-done(((bf16[8,8,1024]{2,1,0:T(8,128)(2,1)}), bf16[8,8,1024]{2,1,0:T(8,128)(2,1)S(1)}, u32[]{:S(2)}, u32[]{:S(2)}) %all-to-all-start) | async-done | bytes 131104 | tf_op jit(solution)/shard_map/all_to_all | solution.py:280
  16.7 0.0 collective-permute-start.1
  17.3 0.7 %collective-permute-done.1.refs_1_ = bf16[8,8,1024]{2,1,0:T(8,128)(2,1)S(1)} collective-permute-done((bf16[8,8,1024]{2,1,0:T(8,128)(2,1)S(1)}, bf16[8,8,1024]{2,1,0:T(8,128)(2,1)S(1)}, u32[]{:S(2)}, u32[]{:S(2)}) %collective-permute-start.1) | collective-permute-done | bytes 131104 | tf_op jit(solution)/shard_map/ppermute | solution.py:272
  18.0 5.1 %tile_work.1 = (f32[8,1024]{1,0:T(8,128)S(1)}, bf16[1,8,1024]{2,1,0:T(8,128)(2,1)S(1)}, f32[32,1,128]{2,1,0:T(1,128)}) custom-call(s32[1]{0:T(128)S(6)} %copy.8.count_s, s32[1024]{0:T(1024)} %rows_h.1, s32[1024]{0:T(1024)} %cols_h.1, f32[1,1024]{1,0:T(1,128)} %bitcast.3, bf16[1024,4096]{1,0:T(8,128)(2,1)} %tiles.1, ...), custom_call_target="tpu_custom_call" | custom-call | flops 67108864 | bytes 8388608 | tf_op jit(solution)/shard_map/tile_work/pallas_call | solution.py:202
  23.1 4.2 %all-to-all-start.1 = ((f32[32,1,128]{2,1,0:T(1,128)}), f32[32,1,128]{2,1,0:T(1,128)S(1)}, u32[]{:S(2)}, u32[]{:S(2)}) async-start(f32[32,1,128]{2,1,0:T(1,128)} %get-tuple-element.10), calls=%async_computation.1 | async-start | bytes 32768 | tf_op jit(solution)/shard_map/all_to_all | solution.py:292
  27.3 1.8 %collective-permute-start.2 = (bf16[8,1024]{1,0:T(8,128)(2,1)S(1)}, bf16[8,1024]{1,0:T(8,128)(2,1)S(1)}, u32[]{:S(2)}, u32[]{:S(2)}) collective-permute-start(bf16[8,1024]{1,0:T(8,128)(2,1)S(1)} %bitcast.2), channel_id=1, source_target_pairs={{0,1},{1,0},{2,3},{3,2},{4,5},{5,4},{6,7},{7,6},{8,9},{9,8},{10,11... | collective-permute-start | bytes 49160 | tf_op jit(solution)/shard_map/ppermute | solution.py:289
  29.1 2.0 %collective-permute-done.2.refs_0_ = bf16[8,1024]{1,0:T(8,128)(2,1)S(1)} collective-permute-done((bf16[8,1024]{1,0:T(8,128)(2,1)S(1)}, bf16[8,1024]{1,0:T(8,128)(2,1)S(1)}, u32[]{:S(2)}, u32[]{:S(2)}) %collective-permute-start.2) | collective-permute-done | bytes 16416 | tf_op jit(solution)/shard_map/ppermute | solution.py:289
  31.1 3.3 %all-to-all-done.1.gram_parts = f32[32,1,128]{2,1,0:T(1,128)S(1)} async-done(((f32[32,1,128]{2,1,0:T(1,128)}), f32[32,1,128]{2,1,0:T(1,128)S(1)}, u32[]{:S(2)}, u32[]{:S(2)}) %all-to-all-start.1) | async-done | bytes 16416 | tf_op jit(solution)/shard_map/all_to_all | solution.py:292
  34.4 0.0 copy-done
  34.4 0.8 %finish.1 = (bf16[8,1024]{1,0:T(8,128)(2,1)}, f32[8,1024]{1,0:T(8,128)}) custom-call(f32[8,1024]{1,0:T(8,128)S(1)} %get-tuple-element.9.base, f32[32,1,128]{2,1,0:T(1,128)S(1)} %all-to-all-done.1.gram_parts, bf16[8,1024]{1,0:T(8,128)(2,1)S(1)} %copy-done, bf16[8,1024]{1,0:T(8,128)(2,1)S(1)} %collective-permute-done.2.refs_0_), custom_call_target="tpu_custom_call" | custom-call | tf_op jit(solution)/shard_map/finish/pallas_call | solution.py:255
Async XLA Ops:
  0.6 33.8 %copy-start = (bf16[8,1024]{1,0:T(8,128)(2,1)S(1)}, bf16[8,1024]{1,0:T(8,128)(2,1)}, u32[]{:S(2)}) copy-start(bf16[8,1024]{1,0:T(8,128)(2,1)} %vec.1) | copy-start | bytes 49156
  2.1 14.6 %all-to-all-start = ((bf16[8,8,1024]{2,1,0:T(8,128)(2,1)}), bf16[8,8,1024]{2,1,0:T(8,128)(2,1)S(1)}, u32[]{:S(2)}, u32[]{:S(2)}) async-start(bf16[8,8,1024]{2,1,0:T(8,128)(2,1)} %broadcast_in_dim.10), calls=%async_computation | async-start | bytes 262144 | tf_op jit(solution)/shard_map/all_to_all | solution.py:280
  9.3 3.9 %collective-permute-start = (bf16[8,1024]{1,0:T(8,128)(2,1)}, bf16[8,1024]{1,0:T(8,128)(2,1)S(1)}, u32[]{:S(2)}, u32[]{:S(2)}) collective-permute-start(bf16[8,1024]{1,0:T(8,128)(2,1)} %vec.1), channel_id=1, source_target_pairs={{0,1},{1,0},{2,3},{3,2},{4,5},{5,4},{6,7},{7,6},{8,9},{9,8},{10,11... | collective-permute-start | bytes 49160 | tf_op jit(solution)/shard_map/ppermute | solution.py:272
  16.7 1.3 %collective-permute-start.1 = (bf16[8,8,1024]{2,1,0:T(8,128)(2,1)S(1)}, bf16[8,8,1024]{2,1,0:T(8,128)(2,1)S(1)}, u32[]{:S(2)}, u32[]{:S(2)}) collective-permute-start(bf16[8,8,1024]{2,1,0:T(8,128)(2,1)S(1)} %all-to-all-done.refs_0_), channel_id=1, source_target_pairs={{0,2},{2,0},{1,3},{3,1},{4,6},{6,4},{5,7},{7,5},{8,10},{10,8},{9,1... | collective-permute-start | bytes 393224 | tf_op jit(solution)/shard_map/ppermute | solution.py:272
  23.1 11.3 %all-to-all-start.1 = ((f32[32,1,128]{2,1,0:T(1,128)}), f32[32,1,128]{2,1,0:T(1,128)S(1)}, u32[]{:S(2)}, u32[]{:S(2)}) async-start(f32[32,1,128]{2,1,0:T(1,128)} %get-tuple-element.10), calls=%async_computation.1 | async-start | bytes 32768 | tf_op jit(solution)/shard_map/all_to_all | solution.py:292
  27.3 3.8 %collective-permute-start.2 = (bf16[8,1024]{1,0:T(8,128)(2,1)S(1)}, bf16[8,1024]{1,0:T(8,128)(2,1)S(1)}, u32[]{:S(2)}, u32[]{:S(2)}) collective-permute-start(bf16[8,1024]{1,0:T(8,128)(2,1)S(1)} %bitcast.2), channel_id=1, source_target_pairs={{0,1},{1,0},{2,3},{3,2},{4,5},{5,4},{6,7},{7,6},{8,9},{9,8},{10,11... | collective-permute-start | bytes 49160 | tf_op jit(solution)/shard_map/ppermute | solution.py:289

commit v6 on v2

--- a/solution.py
+++ b/solution.py
@@ -298,16 +298,18 @@
     base, send, rest = tile_work(
         tile_rows, tile_cols, tile_count, gath, n_col, energies[None, :], tiles
     )
+    others = from_all(vectors, "col")[1:]
+    terms = sum(from_all(gram_terms(base, rest, vectors, others), "core"))
+    send, terms = lax.optimization_barrier((send, terms))
+    members = lax.axis_size(("far", "col"))
+    terms = jnp.broadcast_to(terms[None], (members,) + terms.shape)
+    gram_parts = lax.all_to_all(terms, ("far", "col"), 0, 0)
     got = [
         lax.ppermute(send[s - 1], "col", [(c, (c + s) % n_col) for c in range(n_col)])
         for s in range(1, n_col)
     ]
-    others = from_all(vectors, "col")[1:]
-    members = lax.axis_size(("far", "core", "col"))
-    terms = gram_terms(base, rest, vectors, others)
-    terms = jnp.broadcast_to(terms[None], (members,) + terms.shape)
-    gram_parts = lax.all_to_all(terms, ("far", "core", "col"), 0, 0)
-    return finish(1.0 / (members * own), base, gram_parts, vectors, got)
+    states = lax.axis_size(("far", "core", "col")) * own
+    return finish(1.0 / states, base, gram_parts, vectors, got)
 
 
 def solution(mesh):

time: 34 us -> 36.5 us (1.074)
  blocking collectives: 14.4 us -> 25.5 us
  waiting for transfers between devices: 5.41 us -> 0.89 us
  starting transfers between devices: 5.78 us -> 2.45 us
  local copies, waits for them, and re-layouts: 1.43 us -> 0.8 us
    all_to_all x0 -> x1, blocking collectives: none -> 11.1 us  [per_device(): gram_parts = lax.all_to_all(terms, ('far', 'col'), 0, 0)]
    all_to_all x1 -> x0, waiting for transfers between devices: 3.31 us -> none  [per_device(): gram_parts = lax.all_to_all(terms, ('far', 'core', 'col'), 0, 0)]
    all_to_all x1 -> x0, starting transfers between devices: 2.54 us -> none  [per_device(): gram_parts = lax.all_to_all(terms, ('far', 'core', 'col'), 0, 0)]
    ppermute x1, waiting for transfers between devices: 2.1 us -> 0.01 us  [per_device(): lax.ppermute(send[s - 1], 'col', [(c, (c + s) % n_col) for c in range(n_c...]
    ppermute x1, starting transfers between devices: 1.72 us -> 0.68 us  [per_device(): lax.ppermute(send[s - 1], 'col', [(c, (c + s) % n_col) for c in range(n_c...]
    ppermute x2 -> x3, waiting for transfers between devices: 0.01 us -> 0.89 us  [from_all(): lax.ppermute(x, axis, [(i, (i + s) % size) for i in range(size)])]
    broadcast_in_dim x1, local copies, waits for them, and re-layouts: 0.63 us -> 0.01 us  [per_device(): terms = jnp.broadcast_to(terms[None], (members,) + terms.shape)]
    ppermute x2 -> x3, starting transfers between devices: 1.52 us -> 1.78 us  [from_all(): lax.ppermute(x, axis, [(i, (i + s) % size) for i in range(size)])]
  transfers between devices with their start and end apart: 4 -> 4, of which waited for: 2 -> 1; matrix products, arithmetic and copies ran while one was open for 0% -> 0% of each run, Pallas kernels for 12% -> 11%
where the time goes in v6:
time: 36.5 us; the launch traced here: 36.1 us
  blocking collectives  25.5 us (70%)
  Pallas kernels  5.17 us (14%)
  starting transfers between devices  2.45 us (7%)
  between operations  1.33 us (4%)
  waiting for transfers between devices  0.89 us (2%)
  local copies, waits for them, and re-layouts  0.8 us (2%)
    all_to_all x1, blocking collectives, per_device(): gath = lax.all_to_all(copies, 'far', 0, 0)  14.4 us
    all_to_all x1, blocking collectives, per_device(): gram_parts = lax.all_to_all(terms, ('far', 'col'), 0, 0)  11.1 us
    pallas_call x1, Pallas kernels, tile_work(): pl.pallas_call(functools.partial(tile_kernel, n_core, n_col, side), out_s...  4.12 us
    ppermute x3, starting transfers between devices, from_all(): lax.ppermute(x, axis, [(i, (i + s) % size) for i in range(size)])  1.78 us
    ppermute x3, waiting for transfers between devices, from_all(): lax.ppermute(x, axis, [(i, (i + s) % size) for i in range(size)])  0.89 us
    broadcast_in_dim x1, local copies, waits for them, and re-layouts, per_device(): copies = jnp.broadcast_to(vectors[None], (lax.axis_size('far'), kvec, own))  0.79 us
    pallas_call x1, Pallas kernels, finish(): pl.pallas_call(functools.partial(finish_kernel, scale), out_shape=(jax.Sh...  0.74 us
  transfers between devices with their start and end apart: 4, of which 1 were waited for; matrix products, arithmetic and copies ran while one was open for 0% of the time, Pallas kernels for 11%

profile of v6, /device:TPU:0, one launch (start us, length us, event | category | flops | bytes accessed | tf_op | source)
XLA Modules:
  0.0 36.1 jit_solution(7882226261367495946)
XLA Ops:
  0.6 0.0 copy-start
  0.6 0.8 %broadcast_in_dim.18 = bf16[8,8,1024]{2,1,0:T(8,128)(2,1)S(1)} broadcast(bf16[8,1024]{1,0:T(8,128)(2,1)} %vec.3), dimensions={1,2} | broadcast | bytes 147456 | tf_op jit(solution)/shard_map/broadcast_in_dim | solution.py:295
  1.4 14.4 %all_to_all.10.refs_0_ = bf16[8,8,1024]{2,1,0:T(8,128)(2,1)S(1)} all-to-all(bf16[8,8,1024]{2,1,0:T(8,128)(2,1)S(1)} %broadcast_in_dim.18), channel_id=1, replica_groups=mesh['far'=8,'core'=2,'col'=2] {'far'}, dimensions={0} | all-to-all | bytes 262144 | tf_op jit(solution)/shard_map/all_to_all | solution.py:296
  15.8 0.0 collective-permute-start
  15.8 1.5 %collective-permute-start.1 = (bf16[8,1024]{1,0:T(8,128)(2,1)}, bf16[8,1024]{1,0:T(8,128)(2,1)S(1)}, u32[]{:S(2)}, u32[]{:S(2)}) collective-permute-start(bf16[8,1024]{1,0:T(8,128)(2,1)} %vec.3), channel_id=1, source_target_pairs={{0,1},{1,0},{2,3},{3,2},{4,5},{5,4},{6,7},{7,6},{8,9},{9,8},{10,11... | collective-permute-start | bytes 49160 | tf_op jit(solution)/shard_map/ppermute | solution.py:288
  18.0 0.0 collective-permute-done.refs_1_
  18.0 4.1 %tile_work.1 = (f32[8,1024]{1,0:T(8,128)S(1)}, bf16[1,8,1024]{2,1,0:T(8,128)(2,1)S(1)}, f32[1,8,1024]{2,1,0:T(8,128)S(1)}) custom-call(s32[1]{0:T(128)S(6)} %copy.8.count_s, s32[1024]{0:T(1024)} %rows_h.1, s32[1024]{0:T(1024)} %cols_h.1, f32[1,1024]{1,0:T(1,128)} %bitcast.4, bf16[1024,4096]{1,0:T(8,128)(2,1)} %tiles.1, ...), custom_call_target="tpu_custom_call" | custom-call | flops 67108864 | bytes 8388608 | tf_op jit(solution)/shard_map/tile_work/pallas_call | solution.py:186
  22.1 0.0 collective-permute-done.1.refs_0_
  22.2 0.0 copy-done
  22.2 0.3 gram_terms.1
  22.5 0.3 collective-permute-start.2
  22.7 0.9 %collective-permute-done.2 = f32[1,128]{1,0:T(1,128)S(1)} collective-permute-done((f32[1,128]{1,0:T(1,128)S(1)}, f32[1,128]{1,0:T(1,128)S(1)}, u32[]{:S(2)}, u32[]{:S(2)}) %collective-permute-start.2) | collective-permute-done | bytes 544 | tf_op jit(solution)/shard_map/ppermute | solution.py:288
  23.6 0.7 %collective-permute-start.3 = (bf16[8,1024]{1,0:T(8,128)(2,1)S(1)}, bf16[8,1024]{1,0:T(8,128)(2,1)S(1)}, u32[]{:S(2)}, u32[]{:S(2)}) collective-permute-start(bf16[8,1024]{1,0:T(8,128)(2,1)S(1)} %bitcast.3), channel_id=1, source_target_pairs={{0,1},{1,0},{2,3},{3,2},{4,5},{5,4},{6,7},{7,6},{8,9},{9,8},{10,11... | collective-permute-start | bytes 49160 | tf_op jit(solution)/shard_map/ppermute | solution.py:308
  24.3 11.1 %all_to_all.11.gram_parts = f32[16,1,128]{2,1,0:T(1,128)S(1)} all-to-all(f32[16,1,128]{2,1,0:T(1,128)S(1)} %broadcast_in_dim.20), channel_id=1, replica_groups=mesh['far'=8,'core'=2,'col'=2] {'far','col'}, dimensions={0} | all-to-all | bytes 16384 | tf_op jit(solution)/shard_map/all_to_all | solution.py:306
  35.4 0.0 collective-permute-done.3.refs_0_
  35.4 0.7 %finish.1 = (bf16[8,1024]{1,0:T(8,128)(2,1)}, f32[8,1024]{1,0:T(8,128)}) custom-call(f32[8,1024]{1,0:T(8,128)S(1)} %get-tuple-element.7.own.base, f32[16,1,128]{2,1,0:T(1,128)S(1)} %all_to_all.11.gram_parts, bf16[8,1024]{1,0:T(8,128)(2,1)S(1)} %copy-done, bf16[8,1024]{1,0:T(8,128)(2,1)S(1)} %collective-permute-done.3.refs_0_), custom_call_target="tpu_custom_call" | custom-call | tf_op jit(solution)/shard_map/finish/pallas_call | solution.py:271
  (2 shorter events, 0.0 us)
Async XLA Ops:
  0.6 21.5 %copy-start = (bf16[8,1024]{1,0:T(8,128)(2,1)S(1)}, bf16[8,1024]{1,0:T(8,128)(2,1)}, u32[]{:S(2)}) copy-start(bf16[8,1024]{1,0:T(8,128)(2,1)} %vec.3) | copy-start | bytes 49156
  15.8 2.2 %collective-permute-start = (bf16[8,8,1024]{2,1,0:T(8,128)(2,1)S(1)}, bf16[8,8,1024]{2,1,0:T(8,128)(2,1)S(1)}, u32[]{:S(2)}, u32[]{:S(2)}) collective-permute-start(bf16[8,8,1024]{2,1,0:T(8,128)(2,1)S(1)} %all_to_all.10.refs_0_), channel_id=1, source_target_pairs={{0,2},{2,0},{1,3},{3,1},{4,6},{6,4},{5,7},{7,5},{8,10},{10,8},{9,1... | collective-permute-start | bytes 393224 | tf_op jit(solution)/shard_map/ppermute | solution.py:288
  15.8 6.3 %collective-permute-start.1 = (bf16[8,1024]{1,0:T(8,128)(2,1)}, bf16[8,1024]{1,0:T(8,128)(2,1)S(1)}, u32[]{:S(2)}, u32[]{:S(2)}) collective-permute-start(bf16[8,1024]{1,0:T(8,128)(2,1)} %vec.3), channel_id=1, source_target_pairs={{0,1},{1,0},{2,3},{3,2},{4,5},{5,4},{6,7},{7,6},{8,9},{9,8},{10,11... | collective-permute-start | bytes 49160 | tf_op jit(solution)/shard_map/ppermute | solution.py:288
  22.5 1.1 %collective-permute-start.2 = (f32[1,128]{1,0:T(1,128)S(1)}, f32[1,128]{1,0:T(1,128)S(1)}, u32[]{:S(2)}, u32[]{:S(2)}) collective-permute-start(f32[1,128]{1,0:T(1,128)S(1)} %gram_terms.1), channel_id=1, source_target_pairs={{0,2},{2,0},{1,3},{3,1},{4,6},{6,4},{5,7},{7,5},{8,10},{10,8},{9,1... | collective-permute-start | bytes 1544 | tf_op jit(solution)/shard_map/ppermute | solution.py:288
  23.6 11.8 %collective-permute-start.3 = (bf16[8,1024]{1,0:T(8,128)(2,1)S(1)}, bf16[8,1024]{1,0:T(8,128)(2,1)S(1)}, u32[]{:S(2)}, u32[]{:S(2)}) collective-permute-start(bf16[8,1024]{1,0:T(8,128)(2,1)S(1)} %bitcast.3), channel_id=1, source_target_pairs={{0,1},{1,0},{2,3},{3,2},{4,5},{5,4},{6,7},{7,6},{8,9},{9,8},{10,11... | collective-permute-start | bytes 49160 | tf_op jit(solution)/shard_map/ppermute | solution.py:308

commit v7 on v6

--- a/solution.py
+++ b/solution.py
@@ -252,9 +252,9 @@
     for piece in got:
         whole = whole + piece[...].astype(jnp.float32)
     product[...] = whole.astype(jnp.bfloat16)
-    flat = gram_parts[0]
+    flat = gram_parts[0, :1]
     for i in range(1, gram_parts.shape[0]):
-        flat = flat + gram_parts[i]
+        flat = flat + gram_parts[i, :1]
     kvec = vec.shape[0]
     lane = lax.broadcasted_iota(jnp.int32, (kvec, LANES), 1)
     first = kvec * lax.broadcasted_iota(jnp.int32, (kvec, LANES), 0)
@@ -302,7 +302,7 @@
     terms = sum(from_all(gram_terms(base, rest, vectors, others), "core"))
     send, terms = lax.optimization_barrier((send, terms))
     members = lax.axis_size(("far", "col"))
-    terms = jnp.broadcast_to(terms[None], (members,) + terms.shape)
+    terms = jnp.broadcast_to(terms[None], (members, 4, LANES))
     gram_parts = lax.all_to_all(terms, ("far", "col"), 0, 0)
     got = [
         lax.ppermute(send[s - 1], "col", [(c, (c + s) % n_col) for c in range(n_col)])

time: 36.5 us -> 37.1 us (1.016); the launches traced: 36.1 us -> 37.3 us
  blocking collectives: 25.5 us -> 14.4 us
  waiting for transfers between devices: 0.89 us -> 6.46 us
  starting transfers between devices: 2.45 us -> 7.07 us
  Pallas kernels: 5.17 us -> 6.62 us
  local copies, waits for them, and re-layouts: 0.8 us -> 1.42 us
    all_to_all x1 -> x0, blocking collectives: 11.1 us -> none  [per_device(): gram_parts = lax.all_to_all(terms, ('far', 'col'), 0, 0)]
    all_to_all x0 -> x1, waiting for transfers between devices: none -> 3.55 us  [per_device(): gram_parts = lax.all_to_all(terms, ('far', 'col'), 0, 0)]
    all_to_all x0 -> x1, starting transfers between devices: none -> 3.5 us  [per_device(): gram_parts = lax.all_to_all(terms, ('far', 'col'), 0, 0)]
    ppermute x1, waiting for transfers between devices: 0.01 us -> 2.01 us  [per_device(): lax.ppermute(send[s - 1], 'col', [(c, (c + s) % n_col) for c in range(n_c...]
    pallas_call x1, Pallas kernels: 4.12 us -> 5.57 us  [tile_work(): pl.pallas_call(functools.partial(tile_kernel, n_core, n_col, side), out_s...]
    ppermute x1, starting transfers between devices: 0.68 us -> 1.81 us  [per_device(): lax.ppermute(send[s - 1], 'col', [(c, (c + s) % n_col) for c in range(n_c...]
    broadcast_in_dim x1, local copies, waits for them, and re-layouts: 0.01 us -> 0.62 us  [per_device(): terms = jnp.broadcast_to(terms[None], (members, 4, LANES))]
  transfers between devices with their start and end apart: 4 -> 5, of which waited for: 1 -> 3; matrix products, arithmetic and copies ran while one was open for 0% -> 0% of each run, Pallas kernels for 11% -> 15%
where the time goes in v7:
time: 37.1 us; the launch traced here: 37.3 us
  blocking collectives  14.4 us (39%)
  starting transfers between devices  7.07 us (19%)
  Pallas kernels  6.62 us (18%)
  waiting for transfers between devices  6.46 us (17%)
  local copies, waits for them, and re-layouts  1.42 us (4%)
  between operations  1.34 us (4%)
    all_to_all x1, blocking collectives, per_device(): gath = lax.all_to_all(copies, 'far', 0, 0)  14.4 us
    pallas_call x1, Pallas kernels, tile_work(): pl.pallas_call(functools.partial(tile_kernel, n_core, n_col, side), out_s...  5.57 us
    all_to_all x1, waiting for transfers between devices, per_device(): gram_parts = lax.all_to_all(terms, ('far', 'col'), 0, 0)  3.55 us
    all_to_all x1, starting transfers between devices, per_device(): gram_parts = lax.all_to_all(terms, ('far', 'col'), 0, 0)  3.5 us
    ppermute x1, waiting for transfers between devices, per_device(): lax.ppermute(send[s - 1], 'col', [(c, (c + s) % n_col) for c in range(n_c...  2.01 us
    ppermute x1, starting transfers between devices, per_device(): lax.ppermute(send[s - 1], 'col', [(c, (c + s) % n_col) for c in range(n_c...  1.81 us
    ppermute x3, starting transfers between devices, from_all(): lax.ppermute(x, axis, [(i, (i + s) % size) for i in range(size)])  1.76 us
    ppermute x3, waiting for transfers between devices, from_all(): lax.ppermute(x, axis, [(i, (i + s) % size) for i in range(size)])  0.9 us
  transfers between devices with their start and end apart: 5, of which 3 were waited for; matrix products, arithmetic and copies ran while one was open for 0% of the time, Pallas kernels for 15%

profile of v7, /device:TPU:0, one launch (start us, length us, event | category | flops | bytes accessed | tf_op | source)
XLA Modules:
  0.0 37.3 jit_solution(12261589921574992516)
XLA Ops:
  0.6 0.0 copy-start
  0.6 0.8 %broadcast_in_dim.18 = bf16[8,8,1024]{2,1,0:T(8,128)(2,1)S(1)} broadcast(bf16[8,1024]{1,0:T(8,128)(2,1)} %vec.3), dimensions={1,2} | broadcast | bytes 147456 | tf_op jit(solution)/shard_map/broadcast_in_dim | solution.py:295
  1.4 14.4 %all_to_all.10.refs_0_ = bf16[8,8,1024]{2,1,0:T(8,128)(2,1)S(1)} all-to-all(bf16[8,8,1024]{2,1,0:T(8,128)(2,1)S(1)} %broadcast_in_dim.18), channel_id=1, replica_groups=mesh['far'=8,'core'=2,'col'=2] {'far'}, dimensions={0} | all-to-all | bytes 262144 | tf_op jit(solution)/shard_map/all_to_all | solution.py:296
  15.8 0.0 collective-permute-start
  15.8 1.5 %collective-permute-start.1 = (bf16[8,1024]{1,0:T(8,128)(2,1)}, bf16[8,1024]{1,0:T(8,128)(2,1)S(1)}, u32[]{:S(2)}, u32[]{:S(2)}) collective-permute-start(bf16[8,1024]{1,0:T(8,128)(2,1)} %vec.3), channel_id=1, source_target_pairs={{0,1},{1,0},{2,3},{3,2},{4,5},{5,4},{6,7},{7,6},{8,9},{9,8},{10,11... | collective-permute-start | bytes 49160 | tf_op jit(solution)/shard_map/ppermute | solution.py:288
  18.0 0.0 collective-permute-done.refs_1_
  18.0 5.6 %tile_work.1 = (f32[8,1024]{1,0:T(8,128)S(1)}, bf16[1,8,1024]{2,1,0:T(8,128)(2,1)S(1)}, f32[1,8,1024]{2,1,0:T(8,128)S(1)}) custom-call(s32[1]{0:T(128)S(6)} %copy.8.count_s, s32[1024]{0:T(1024)} %rows_h.1, s32[1024]{0:T(1024)} %cols_h.1, f32[1,1024]{1,0:T(1,128)} %bitcast.4, bf16[1024,4096]{1,0:T(8,128)(2,1)} %tiles.1, ...), custom_call_target="tpu_custom_call" | custom-call | flops 67108864 | bytes 8388608 | tf_op jit(solution)/shard_map/tile_work/pallas_call | solution.py:186
  23.6 0.0 collective-permute-done.1.refs_0_
  23.6 0.0 copy-done
  23.6 0.3 gram_terms.1
  23.9 0.2 collective-permute-start.2
  24.2 0.9 %collective-permute-done.2 = f32[1,128]{1,0:T(1,128)S(1)} collective-permute-done((f32[1,128]{1,0:T(1,128)S(1)}, f32[1,128]{1,0:T(1,128)S(1)}, u32[]{:S(2)}, u32[]{:S(2)}) %collective-permute-start.2) | collective-permute-done | bytes 544 | tf_op jit(solution)/shard_map/ppermute | solution.py:288
  25.1 0.6 %broadcast_in_dim.20 = f32[16,4,128]{2,1,0:T(4,128)} broadcast(f32[128]{0:T(128)S(1)} %bitcast.5), dimensions={2} | broadcast | bytes 33280 | tf_op jit(solution)/shard_map/broadcast_in_dim | solution.py:305
  25.7 3.5 %all-to-all-start.1 = ((f32[16,4,128]{2,1,0:T(4,128)}), f32[16,4,128]{2,1,0:T(4,128)S(1)}, u32[]{:S(2)}, u32[]{:S(2)}) async-start(f32[16,4,128]{2,1,0:T(4,128)} %broadcast_in_dim.20), calls=%async_computation.1 | async-start | bytes 65536 | tf_op jit(solution)/shard_map/all_to_all | solution.py:306
  29.2 1.8 %collective-permute-start.3 = (bf16[8,1024]{1,0:T(8,128)(2,1)S(1)}, bf16[8,1024]{1,0:T(8,128)(2,1)S(1)}, u32[]{:S(2)}, u32[]{:S(2)}) collective-permute-start(bf16[8,1024]{1,0:T(8,128)(2,1)S(1)} %bitcast.3), channel_id=1, source_target_pairs={{0,1},{1,0},{2,3},{3,2},{4,5},{5,4},{6,7},{7,6},{8,9},{9,8},{10,11... | collective-permute-start | bytes 49160 | tf_op jit(solution)/shard_map/ppermute | solution.py:308
  31.0 2.0 %collective-permute-done.3.refs_0_ = bf16[8,1024]{1,0:T(8,128)(2,1)S(1)} collective-permute-done((bf16[8,1024]{1,0:T(8,128)(2,1)S(1)}, bf16[8,1024]{1,0:T(8,128)(2,1)S(1)}, u32[]{:S(2)}, u32[]{:S(2)}) %collective-permute-start.3) | collective-permute-done | bytes 16416 | tf_op jit(solution)/shard_map/ppermute | solution.py:308
  33.0 3.6 %all-to-all-done.1.gram_parts = f32[16,4,128]{2,1,0:T(4,128)S(1)} async-done(((f32[16,4,128]{2,1,0:T(4,128)}), f32[16,4,128]{2,1,0:T(4,128)S(1)}, u32[]{:S(2)}, u32[]{:S(2)}) %all-to-all-start.1) | async-done | bytes 32800 | tf_op jit(solution)/shard_map/all_to_all | solution.py:306
  36.6 0.7 %finish.1 = (bf16[8,1024]{1,0:T(8,128)(2,1)}, f32[8,1024]{1,0:T(8,128)}) custom-call(f32[8,1024]{1,0:T(8,128)S(1)} %get-tuple-element.7.own.base, f32[16,4,128]{2,1,0:T(4,128)S(1)} %all-to-all-done.1.gram_parts, bf16[8,1024]{1,0:T(8,128)(2,1)S(1)} %copy-done, bf16[8,1024]{1,0:T(8,128)(2,1)S(1)} %collective-permute-done.3.refs_0_), custom_call_target="tpu_custom_call" | custom-call | tf_op jit(solution)/shard_map/finish/pallas_call | solution.py:271
  (1 shorter events, 0.0 us)
Async XLA Ops:
  0.6 23.0 %copy-start = (bf16[8,1024]{1,0:T(8,128)(2,1)S(1)}, bf16[8,1024]{1,0:T(8,128)(2,1)}, u32[]{:S(2)}) copy-start(bf16[8,1024]{1,0:T(8,128)(2,1)} %vec.3) | copy-start | bytes 49156
  15.8 2.2 %collective-permute-start = (bf16[8,8,1024]{2,1,0:T(8,128)(2,1)S(1)}, bf16[8,8,1024]{2,1,0:T(8,128)(2,1)S(1)}, u32[]{:S(2)}, u32[]{:S(2)}) collective-permute-start(bf16[8,8,1024]{2,1,0:T(8,128)(2,1)S(1)} %all_to_all.10.refs_0_), channel_id=1, source_target_pairs={{0,2},{2,0},{1,3},{3,1},{4,6},{6,4},{5,7},{7,5},{8,10},{10,8},{9,1... | collective-permute-start | bytes 393224 | tf_op jit(solution)/shard_map/ppermute | solution.py:288
  15.8 7.8 %collective-permute-start.1 = (bf16[8,1024]{1,0:T(8,128)(2,1)}, bf16[8,1024]{1,0:T(8,128)(2,1)S(1)}, u32[]{:S(2)}, u32[]{:S(2)}) collective-permute-start(bf16[8,1024]{1,0:T(8,128)(2,1)} %vec.3), channel_id=1, source_target_pairs={{0,1},{1,0},{2,3},{3,2},{4,5},{5,4},{6,7},{7,6},{8,9},{9,8},{10,11... | collective-permute-start | bytes 49160 | tf_op jit(solution)/shard_map/ppermute | solution.py:288
  23.9 1.1 %collective-permute-start.2 = (f32[1,128]{1,0:T(1,128)S(1)}, f32[1,128]{1,0:T(1,128)S(1)}, u32[]{:S(2)}, u32[]{:S(2)}) collective-permute-start(f32[1,128]{1,0:T(1,128)S(1)} %gram_terms.1), channel_id=1, source_target_pairs={{0,2},{2,0},{1,3},{3,1},{4,6},{6,4},{5,7},{7,5},{8,10},{10,8},{9,1... | collective-permute-start | bytes 1544 | tf_op jit(solution)/shard_map/ppermute | solution.py:288
  25.7 10.9 %all-to-all-start.1 = ((f32[16,4,128]{2,1,0:T(4,128)}), f32[16,4,128]{2,1,0:T(4,128)S(1)}, u32[]{:S(2)}, u32[]{:S(2)}) async-start(f32[16,4,128]{2,1,0:T(4,128)} %broadcast_in_dim.20), calls=%async_computation.1 | async-start | bytes 65536 | tf_op jit(solution)/shard_map/all_to_all | solution.py:306
  29.2 3.8 %collective-permute-start.3 = (bf16[8,1024]{1,0:T(8,128)(2,1)S(1)}, bf16[8,1024]{1,0:T(8,128)(2,1)S(1)}, u32[]{:S(2)}, u32[]{:S(2)}) collective-permute-start(bf16[8,1024]{1,0:T(8,128)(2,1)S(1)} %bitcast.3), channel_id=1, source_target_pairs={{0,1},{1,0},{2,3},{3,2},{4,5},{5,4},{6,7},{7,6},{8,9},{9,8},{10,11... | collective-permute-start | bytes 49160 | tf_op jit(solution)/shard_map/ppermute | solution.py:308

commit v8 on v2

--- a/solution.py
+++ b/solution.py
@@ -103,15 +103,19 @@
             slot = base + half * SUB + t
             at = cols_s[slot]
             entries.append(table[jnp.where(slot < count, at, n_blocks) if check else at])
-        left = jnp.concatenate(entries, axis=0).astype(jnp.bfloat16)
-        return lax.dot_general(left, w, NT, preferred_element_type=jnp.float32)
+        outs = []
+        for i in range(0, SUB, SUB // 2):
+            left = jnp.concatenate(entries[i:i + SUB // 2], axis=0).astype(jnp.bfloat16)
+            out = lax.dot_general(left, w, NT, preferred_element_type=jnp.float32)
+            outs += [out[t * rows_of:(t + 1) * rows_of] for t in range(SUB // 2)]
+        return outs
 
     lane_w = lax.broadcasted_iota(jnp.int32, (rows_of, width), 1) % SUB
 
     def accumulate(at, out):
         for t in range(SUB):
             r = rows_s[at + t]
-            mine = jnp.where(lane_w == t, out[t * rows_of:(t + 1) * rows_of], 0.0)
+            mine = jnp.where(lane_w == t, out[t], 0.0)
             acc[t % len(acc)][r] += mine
 
     def step(first, slots_in, check):

time: 34 us -> 36.5 us (1.074)
  starting transfers between devices: 5.78 us -> 8.05 us
  Pallas kernels: 5.2 us -> 5.75 us
    all_to_all x1, starting transfers between devices: 2.54 us -> 4.7 us  [per_device(): gram_parts = lax.all_to_all(terms, ('far', 'core', 'col'), 0, 0)]
    pallas_call x1, Pallas kernels: 4.13 us -> 4.68 us  [tile_work(): pl.pallas_call(functools.partial(tile_kernel, n_core, n_col, side), out_s...]
  transfers between devices with their start and end apart: 4 -> 4, of which waited for: 2 -> 2; matrix products, arithmetic and copies ran while one was open for 0% -> 0% of each run, Pallas kernels for 12% -> 13%
where the time goes in v8:
time: 36.5 us; the launch traced here: 36.3 us
  blocking collectives  14.4 us (39%)
  starting transfers between devices  8.05 us (22%)
  Pallas kernels  5.75 us (16%)
  waiting for transfers between devices  5.29 us (14%)
  local copies, waits for them, and re-layouts  1.43 us (4%)
  between operations  1.33 us (4%)
    all_to_all x1, blocking collectives, per_device(): gath = lax.all_to_all(copies, 'far', 0, 0)  14.4 us
    all_to_all x1, starting transfers between devices, per_device(): gram_parts = lax.all_to_all(terms, ('far', 'core', 'col'), 0, 0)  4.7 us
    pallas_call x1, Pallas kernels, tile_work(): pl.pallas_call(functools.partial(tile_kernel, n_core, n_col, side), out_s...  4.68 us
    all_to_all x1, waiting for transfers between devices, per_device(): gram_parts = lax.all_to_all(terms, ('far', 'core', 'col'), 0, 0)  3.3 us
    ppermute x1, waiting for transfers between devices, per_device(): lax.ppermute(send[s - 1], 'col', [(c, (c + s) % n_col) for c in range(n_c...  1.99 us
    ppermute x1, starting transfers between devices, per_device(): lax.ppermute(send[s - 1], 'col', [(c, (c + s) % n_col) for c in range(n_c...  1.83 us
    ppermute x2, starting transfers between devices, from_all(): lax.ppermute(x, axis, [(i, (i + s) % size) for i in range(size)])  1.52 us
    broadcast_in_dim x1, local copies, waits for them, and re-layouts, per_device(): copies = jnp.broadcast_to(vectors[None], (lax.axis_size('far'), kvec, own))  0.79 us
  transfers between devices with their start and end apart: 4, of which 2 were waited for; matrix products, arithmetic and copies ran while one was open for 0% of the time, Pallas kernels for 13%

profile of v8, /device:TPU:0, one launch (start us, length us, event | category | flops | bytes accessed | tf_op | source)
XLA Modules:
  0.0 36.3 jit_solution(14964717928179354840)
XLA Ops:
  0.6 0.0 copy-start
  0.6 0.8 %broadcast_in_dim.18 = bf16[8,8,1024]{2,1,0:T(8,128)(2,1)S(1)} broadcast(bf16[8,1024]{1,0:T(8,128)(2,1)} %vec.3), dimensions={1,2} | broadcast | bytes 147456 | tf_op jit(solution)/shard_map/broadcast_in_dim | solution.py:299
  1.4 14.4 %all_to_all.10.refs_0_ = bf16[8,8,1024]{2,1,0:T(8,128)(2,1)S(1)} all-to-all(bf16[8,8,1024]{2,1,0:T(8,128)(2,1)S(1)} %broadcast_in_dim.18), channel_id=1, replica_groups=mesh['far'=8,'core'=2,'col'=2] {'far'}, dimensions={0} | all-to-all | bytes 262144 | tf_op jit(solution)/shard_map/all_to_all | solution.py:300
  15.8 0.0 collective-permute-start
  15.8 1.5 %collective-permute-start.1 = (bf16[8,1024]{1,0:T(8,128)(2,1)}, bf16[8,1024]{1,0:T(8,128)(2,1)S(1)}, u32[]{:S(2)}, u32[]{:S(2)}) collective-permute-start(bf16[8,1024]{1,0:T(8,128)(2,1)} %vec.3), channel_id=1, source_target_pairs={{0,1},{1,0},{2,3},{3,2},{4,5},{5,4},{6,7},{7,6},{8,9},{9,8},{10,11... | collective-permute-start | bytes 49160 | tf_op jit(solution)/shard_map/ppermute | solution.py:292
  18.0 0.0 collective-permute-done.refs_1_
  18.0 4.7 %tile_work.1 = (f32[8,1024]{1,0:T(8,128)S(1)}, bf16[1,8,1024]{2,1,0:T(8,128)(2,1)S(1)}, f32[1,8,1024]{2,1,0:T(8,128)S(1)}) custom-call(s32[1]{0:T(128)S(6)} %copy.8.count_s, s32[1024]{0:T(1024)} %rows_h.1, s32[1024]{0:T(1024)} %cols_h.1, f32[1,1024]{1,0:T(1,128)} %bitcast.5, bf16[1024,4096]{1,0:T(8,128)(2,1)} %tiles.1, ...), custom_call_target="tpu_custom_call" | custom-call | flops 67108864 | bytes 8388608 | tf_op jit(solution)/shard_map/tile_work/pallas_call | solution.py:190
  22.7 0.0 collective-permute-done.1.refs_0_
  22.7 0.0 copy-done
  22.7 0.3 gram_terms.1
  23.0 0.6 %broadcast_in_dim.20 = f32[32,1,128]{2,1,0:T(1,128)} broadcast(f32[128]{0:T(128)S(1)} %bitcast.3), dimensions={2} | broadcast | bytes 16896 | tf_op jit(solution)/shard_map/broadcast_in_dim | solution.py:312
  23.7 4.7 %all-to-all-start.1 = ((f32[32,1,128]{2,1,0:T(1,128)}), f32[32,1,128]{2,1,0:T(1,128)S(1)}, u32[]{:S(2)}, u32[]{:S(2)}) async-start(f32[32,1,128]{2,1,0:T(1,128)} %broadcast_in_dim.20), calls=%async_computation.1 | async-start | bytes 32768 | tf_op jit(solution)/shard_map/all_to_all | solution.py:313
  28.4 1.8 %collective-permute-start.2 = (bf16[8,1024]{1,0:T(8,128)(2,1)S(1)}, bf16[8,1024]{1,0:T(8,128)(2,1)S(1)}, u32[]{:S(2)}, u32[]{:S(2)}) collective-permute-start(bf16[8,1024]{1,0:T(8,128)(2,1)S(1)} %bitcast.4), channel_id=1, source_target_pairs={{0,1},{1,0},{2,3},{3,2},{4,5},{5,4},{6,7},{7,6},{8,9},{9,8},{10,11... | collective-permute-start | bytes 49160 | tf_op jit(solution)/shard_map/ppermute | solution.py:306
  30.2 2.0 %collective-permute-done.2.refs_0_ = bf16[8,1024]{1,0:T(8,128)(2,1)S(1)} collective-permute-done((bf16[8,1024]{1,0:T(8,128)(2,1)S(1)}, bf16[8,1024]{1,0:T(8,128)(2,1)S(1)}, u32[]{:S(2)}, u32[]{:S(2)}) %collective-permute-start.2) | collective-permute-done | bytes 16416 | tf_op jit(solution)/shard_map/ppermute | solution.py:306
  32.2 3.3 %all-to-all-done.1.gram_parts = f32[32,1,128]{2,1,0:T(1,128)S(1)} async-done(((f32[32,1,128]{2,1,0:T(1,128)}), f32[32,1,128]{2,1,0:T(1,128)S(1)}, u32[]{:S(2)}, u32[]{:S(2)}) %all-to-all-start.1) | async-done | bytes 16416 | tf_op jit(solution)/shard_map/all_to_all | solution.py:313
  35.5 0.8 %finish.1 = (bf16[8,1024]{1,0:T(8,128)(2,1)}, f32[8,1024]{1,0:T(8,128)}) custom-call(f32[8,1024]{1,0:T(8,128)S(1)} %get-tuple-element.5.own.base, f32[32,1,128]{2,1,0:T(1,128)S(1)} %all-to-all-done.1.gram_parts, bf16[8,1024]{1,0:T(8,128)(2,1)S(1)} %copy-done, bf16[8,1024]{1,0:T(8,128)(2,1)S(1)} %collective-permute-done.2.refs_0_), custom_call_target="tpu_custom_call" | custom-call | tf_op jit(solution)/shard_map/finish/pallas_call | solution.py:275
Async XLA Ops:
  0.6 22.1 %copy-start = (bf16[8,1024]{1,0:T(8,128)(2,1)S(1)}, bf16[8,1024]{1,0:T(8,128)(2,1)}, u32[]{:S(2)}) copy-start(bf16[8,1024]{1,0:T(8,128)(2,1)} %vec.3) | copy-start | bytes 49156
  15.8 2.2 %collective-permute-start = (bf16[8,8,1024]{2,1,0:T(8,128)(2,1)S(1)}, bf16[8,8,1024]{2,1,0:T(8,128)(2,1)S(1)}, u32[]{:S(2)}, u32[]{:S(2)}) collective-permute-start(bf16[8,8,1024]{2,1,0:T(8,128)(2,1)S(1)} %all_to_all.10.refs_0_), channel_id=1, source_target_pairs={{0,2},{2,0},{1,3},{3,1},{4,6},{6,4},{5,7},{7,5},{8,10},{10,8},{9,1... | collective-permute-start | bytes 393224 | tf_op jit(solution)/shard_map/ppermute | solution.py:292
  15.8 6.9 %collective-permute-start.1 = (bf16[8,1024]{1,0:T(8,128)(2,1)}, bf16[8,1024]{1,0:T(8,128)(2,1)S(1)}, u32[]{:S(2)}, u32[]{:S(2)}) collective-permute-start(bf16[8,1024]{1,0:T(8,128)(2,1)} %vec.3), channel_id=1, source_target_pairs={{0,1},{1,0},{2,3},{3,2},{4,5},{5,4},{6,7},{7,6},{8,9},{9,8},{10,11... | collective-permute-start | bytes 49160 | tf_op jit(solution)/shard_map/ppermute | solution.py:292
  23.7 11.8 %all-to-all-start.1 = ((f32[32,1,128]{2,1,0:T(1,128)}), f32[32,1,128]{2,1,0:T(1,128)S(1)}, u32[]{:S(2)}, u32[]{:S(2)}) async-start(f32[32,1,128]{2,1,0:T(1,128)} %broadcast_in_dim.20), calls=%async_computation.1 | async-start | bytes 32768 | tf_op jit(solution)/shard_map/all_to_all | solution.py:313
  28.4 3.8 %collective-permute-start.2 = (bf16[8,1024]{1,0:T(8,128)(2,1)S(1)}, bf16[8,1024]{1,0:T(8,128)(2,1)S(1)}, u32[]{:S(2)}, u32[]{:S(2)}) collective-permute-start(bf16[8,1024]{1,0:T(8,128)(2,1)S(1)} %bitcast.4), channel_id=1, source_target_pairs={{0,1},{1,0},{2,3},{3,2},{4,5},{5,4},{6,7},{7,6},{8,9},{9,8},{10,11... | collective-permute-start | bytes 49160 | tf_op jit(solution)/shard_map/ppermute | solution.py:306
